TPU v7x, 128 devices: a whole 4x4x4 slice. The times are simulated.
128 devices in a mesh: rows: 32 (over z, x, core), half: 4 (over y).
Axes of the slice: x: 4, y: 4, z: 4, core: 2. Of those that a mesh axis runs over, the one named last changes fastest.
Arguments:
- pair: bfloat16 [1024, 1024, 128], P('rows', 'half'), may hold values from -6 to 6
- pair_mask: int32 [1024, 1024], P('rows', 'half'), may hold values from 0 to 1, as said below
- gains: float32 [3, 128], replicated, may hold values from 0.1 to 1.9
- w_tri: bfloat16 [128, 640], replicated, may hold values from -0.5 to 0.5
- w_tri_out: bfloat16 [128, 128], replicated, may hold values from -0.5 to 0.5
- w_att: bfloat16 [128, 512], replicated, may hold values from -0.5 to 0.5
- w_bias: bfloat16 [128, 4], replicated, may hold values from -0.5 to 0.5
- w_att_out: bfloat16 [128, 128], replicated, may hold values from -0.5 to 0.5
Outputs:
- updated: bfloat16 [1024, 1024, 128], P('rows', 'half')
Inputs may be any that keep to these rules, and one draw needn't show every extreme that they name: The last tokens of the crop are padding, between 102 and 2 * (102) of them: pair_mask[i, k] is 0 wherever token i or token k is padding. Other pairs may be 0 as well.
All inputs are finite; a program needn't handle non-finite values.
Results may differ from a plain program's by a relative error of at most 0.012.
Values may be sent and summed in bfloat16 or wider, within the bound.
No kernel may reach another device: no remote copies, remote signals or barrier semaphores. Data moves between devices by JAX's collectives and lax.ppermute only.
A program may use at most 128 MiB of HBM per device.

v0:
```python
import functools

import jax
import jax.numpy as jnp
from jax import lax
from jax.experimental import pallas as pl
from jax.experimental.pallas import tpu as pltpu
from jax.sharding import PartitionSpec as P

LOG2E = 1.4426950408889634
NEG = -1e30
SAFE = 100.0
AXES = ("rows", "half")
VMEM = pl.BlockSpec(memory_space=pltpu.VMEM)
SMEM = pl.BlockSpec(memory_space=pltpu.SMEM)
PARAMS = pltpu.CompilerParams(vmem_limit_bytes=62 << 20)
CHUNKS = 2


def dot_nn(a, b):
    return lax.dot_general(a, b, (((1,), (0,)), ((), ())), preferred_element_type=jnp.float32)


def dot_nt(a, b):
    return lax.dot_general(a, b, (((1,), (1,)), ((), ())), preferred_element_type=jnp.float32)


def dot_tn(a, b):
    return lax.dot_general(a, b, (((0,), (0,)), ((), ())), preferred_element_type=jnp.float32)


def sigmoid(x):
    return 0.5 * jnp.tanh(0.5 * x) + 0.5


def norm_lanes(x, gain):
    x = x.astype(jnp.float32)
    center = x - jnp.mean(x, axis=-1, keepdims=True)
    spread = jnp.mean(center * center, axis=-1, keepdims=True)
    return (center * lax.rsqrt(spread + 1e-05) * gain).astype(jnp.bfloat16)


def norm_sublanes(x, gain):
    x = x.astype(jnp.float32)
    center = x - jnp.mean(x, axis=0, keepdims=True)
    spread = jnp.mean(center * center, axis=0, keepdims=True)
    return (center * lax.rsqrt(spread + 1e-05) * gain).astype(jnp.bfloat16)


def edges_kernel(pair_ref, mask_ref, gain_ref, w_ref, out_ref, scr):
    group, cols, width = pair_ref.shape
    gain = gain_ref[0:1, :]
    wt = w_ref[:, : 4 * width].T

    def some(t, carry):
        x = pair_ref[pl.ds(t * EDGE_ROWS, EDGE_ROWS)].reshape(EDGE_ROWS * cols, width)
        mixed = dot_nt(wt, norm_lanes(x, gain))
        m = jnp.concatenate(
            [mask_ref[pl.ds(t * EDGE_ROWS + r, 1), :] for r in range(EDGE_ROWS)], axis=1
        ).astype(jnp.float32)
        left = m * sigmoid(mixed[width : 2 * width]) * mixed[:width]
        right = m * sigmoid(mixed[3 * width :]) * mixed[2 * width : 3 * width]
        for e, edge in enumerate((left, right)):
            for r in range(EDGE_ROWS):
                for s in range(cols // 128):
                    at = r * cols + s * 128
                    scr[e, s, pl.ds(t * EDGE_ROWS + r, width, stride=group), :] = edge[:, at : at + 128]
        return carry

    lax.fori_loop(0, group // EDGE_ROWS, some, 0, unroll=EDGE_UNROLL)
    for e in range(2):
        for s in range(cols // 128):
            out_ref[:, e, :, s * 128 : (s + 1) * 128] = (
                scr[e, s].reshape(width, group, 128).astype(jnp.bfloat16)
            )


EDGE_UNROLL = 1
EDGE_ROWS = 8


def edges(pair, mask, gains, w, group=8):
    rows, cols, width = pair.shape
    return pl.pallas_call(
        edges_kernel,
        grid=(rows // group,),
        out_shape=jax.ShapeDtypeStruct((width, 2, rows, cols), jnp.bfloat16),
        in_specs=[
            pl.BlockSpec((group, cols, width), lambda i: (i, 0, 0)),
            pl.BlockSpec((group, cols), lambda i: (i, 0)),
            VMEM,
            VMEM,
        ],
        out_specs=pl.BlockSpec((width, 2, group, cols), lambda i: (0, 0, i, 0)),
        scratch_shapes=[pltpu.VMEM((2, cols // 128, width * group, 128), jnp.float32)],
        compiler_params=PARAMS,
    )(pair, mask, gains, w)


def gate_kernel(pair_ref, gain_ref, w_ref, out_ref):
    group, cols, width = pair_ref.shape
    normed = norm_lanes(pair_ref[...].reshape(group * cols, width), gain_ref[0:1, :])
    gates = sigmoid(dot_nn(normed, w_ref[:, 4 * width :])).astype(jnp.bfloat16)
    out_ref[...] = gates.reshape(group, cols, width)


def gate(pair, gains, w, group=8):
    rows, cols, width = pair.shape
    block = pl.BlockSpec((group, cols, width), lambda i: (i, 0, 0))
    return pl.pallas_call(
        gate_kernel,
        grid=(rows // group,),
        out_shape=jax.ShapeDtypeStruct(pair.shape, jnp.bfloat16),
        in_specs=[block, VMEM, VMEM],
        out_specs=block,
        compiler_params=PARAMS,
        cost_estimate=pl.CostEstimate(
            flops=6 * rows * cols * width * width,
            bytes_accessed=4 * rows * cols * width,
            transcendentals=rows * cols * width,
        ),
    )(pair, gains, w)


PRODUCT_ROWS = 512


def product_kernel(lr_ref, out_ref):
    blocks, halves, _, rows, cols = lr_ref.shape
    step = PRODUCT_ROWS // rows

    def tile(t, carry):
        acc = None
        for h in range(halves):
            left = lr_ref[pl.ds(t * step, step), h, 0].reshape(step * rows, cols)
            right = lr_ref[:, h, 1].reshape(blocks * rows, cols)
            part = dot_nt(left, right)
            acc = part if acc is None else acc + part
        for h in range(halves):
            out_ref[pl.ds(t * step, step), h] = (
                acc[:, h * cols : (h + 1) * cols].reshape(step, rows, cols).astype(jnp.bfloat16)
            )
        return carry

    lax.fori_loop(0, blocks // step, tile, 0)


def product(lr):
    blocks, halves, _, rows, cols = lr.shape
    return pl.pallas_call(
        product_kernel,
        out_shape=jax.ShapeDtypeStruct((blocks, halves, rows, cols), jnp.bfloat16),
        in_specs=[VMEM],
        out_specs=VMEM,
        compiler_params=PARAMS,
    )(lr)


OUT_ROWS = 8


def output_kernel(prod_ref, pair_ref, gate_ref, mask_ref, gain_ref, gcol_ref, wo_ref, wb_ref, after_ref, norm_ref, bias_ref, scr):
    width, rows, cols = prod_ref.shape
    heads = bias_ref.shape[1]
    for s in range(cols // 128):
        for c in range(0, width, 16):
            part = prod_ref[c : c + 16, :, s * 128 : (s + 1) * 128].astype(jnp.float32)
            scr[s, c * rows : (c + 16) * rows, :] = part.reshape(16 * rows, 128)

    def some(t, carry):
        i = t * OUT_ROWS
        x = jnp.concatenate(
            [
                scr[s, pl.ds(i + r, width, stride=rows), :]
                for r in range(OUT_ROWS)
                for s in range(cols // 128)
            ],
            axis=1,
        )
        normed = norm_sublanes(x.astype(jnp.bfloat16), gcol_ref[...])
        update = dot_tn(normed, wo_ref[...])
        here = pl.ds(i, OUT_ROWS)
        flat = (OUT_ROWS * cols, width)
        p = pair_ref[here].reshape(flat).astype(jnp.float32)
        after = p + gate_ref[here].reshape(flat).astype(jnp.float32) * update
        after = after.astype(jnp.bfloat16)
        after_ref[here] = after.reshape(OUT_ROWS, cols, width)
        a = norm_lanes(after, gain_ref[2:3, :])
        norm_ref[here] = a.reshape(OUT_ROWS, cols, width)
        bias = (dot_nt(wb_ref[...], a) * LOG2E).astype(jnp.bfloat16)
        for r in range(OUT_ROWS):
            bias_ref[i + r] = bias[:heads, r * cols : (r + 1) * cols]
        return carry

    lax.fori_loop(0, rows // OUT_ROWS, some, 0)
    used = rows * cols // width
    norm_ref[rows, :used, :] = mask_ref[...]
    norm_ref[rows, used:, :] = jnp.zeros((cols - used, width), jnp.bfloat16)


def tri_output(prod, pair, gates, mask_flat, gains, gcol, wo, wb, heads, chunk):
    width, rows, cols = prod.shape
    rows //= CHUNKS
    block = pl.BlockSpec((rows, cols, width), lambda i: (chunk, 0, 0))
    return pl.pallas_call(
        output_kernel,
        grid=(1,),
        out_shape=(
            jax.ShapeDtypeStruct((rows, cols, width), jnp.bfloat16),
            jax.ShapeDtypeStruct((rows + 1, cols, width), jnp.bfloat16),
            jax.ShapeDtypeStruct((rows, heads, cols), jnp.bfloat16),
        ),
        in_specs=[
            pl.BlockSpec((width, rows, cols), lambda i: (0, chunk, 0)),
            block,
            block,
            pl.BlockSpec((rows * cols // width, width), lambda i: (chunk, 0)),
        ]
        + [VMEM] * 4,
        out_specs=(VMEM,) * 3,
        scratch_shapes=[pltpu.VMEM((cols // 128, width * rows, 128), jnp.float32)],
        compiler_params=PARAMS,
    )(prod, pair, gates, mask_flat, gains, gcol, wo, wb)


def project_kernel(w_ref, *refs):
    width = w_ref.shape[0]
    xs = refs[:-5]
    q_ref, g_ref, k_ref, v_ref, m_ref = refs[-5:]
    group, cols, _ = xs[0].shape
    scale = LOG2E * HEAD_DIM**-0.5
    tops = [None] * group
    for b, x_ref in enumerate(xs):
        a = x_ref[...].reshape(group * cols, width)
        at = slice(b * cols, (b + 1) * cols)
        if b == 0:
            mixed = dot_nn(a, w_ref[...])
            q_ref[...] = (mixed[:, :width] * scale).astype(jnp.bfloat16).reshape(q_ref.shape)
            g_ref[...] = sigmoid(mixed[:, 3 * width :]).astype(jnp.bfloat16).reshape(g_ref.shape)
            kv = mixed[:, width : 3 * width].astype(jnp.bfloat16)
        else:
            kv = dot_nn(a, w_ref[:, width : 3 * width]).astype(jnp.bfloat16)
        k_ref[:, at, :] = kv[:, :width].reshape(group, cols, width)
        v_ref[:, at, :] = kv[:, width:].reshape(group, cols, width)
        for r in range(group):
            m = jnp.max(jnp.abs(kv[r * cols : (r + 1) * cols, :width]), axis=0, keepdims=True)
            tops[r] = m if tops[r] is None else jnp.maximum(tops[r], m)
    for r in range(group):
        m_ref[r] = jnp.broadcast_to(tops[r].astype(jnp.float32), m_ref.shape[1:])


HEAD_DIM = 32
AHEAD = 1


def project(blocks, w, group=8):
    rows, cols, width = blocks[0].shape
    rows -= 1
    n = len(blocks)
    one = lambda c: pl.BlockSpec((group, c, width), lambda i: (i, 0, 0))
    shape = lambda c: jax.ShapeDtypeStruct((rows, c, width), jnp.bfloat16)
    return pl.pallas_call(
        project_kernel,
        grid=(rows // group,),
        out_shape=(shape(cols), shape(cols), shape(n * cols), shape(n * cols), jax.ShapeDtypeStruct((rows, 8, width), jnp.float32)),
        in_specs=[VMEM] + [one(cols)] * n,
        out_specs=(one(cols), one(cols), one(n * cols), one(n * cols), one(8)),
        compiler_params=PARAMS,
        cost_estimate=pl.CostEstimate(
            flops=8 * n * rows * cols * width * width,
            bytes_accessed=8 * n * rows * cols * width,
            transcendentals=rows * cols * width,
        ),
    )(w, *blocks)


def project_last_kernel(w_ref, e_ref, x_ref, q_ref, top_ref, k_ref, v_ref, m_ref):
    width = w_ref.shape[0]
    group, cols, _ = x_ref.shape
    a = x_ref[...].reshape(group * cols, width)
    kv = dot_nn(a, w_ref[:, width : 3 * width]).astype(jnp.bfloat16)
    k_ref[...] = kv[:, :width].reshape(k_ref.shape)
    v_ref[...] = kv[:, width:].reshape(v_ref.shape)
    sized = []
    for r in range(group):
        m = jnp.max(jnp.abs(kv[r * cols : (r + 1) * cols, :width]), axis=0, keepdims=True)
        top = jnp.maximum(m.astype(jnp.float32), top_ref[r, 0:1, :])
        sized.append((jnp.abs(q_ref[r]).astype(jnp.float32) * top).astype(jnp.bfloat16))
    reach = dot_nn(jnp.concatenate(sized, axis=0), e_ref[...])
    for r in range(group):
        m = jnp.max(reach[r * cols : (r + 1) * cols], axis=0, keepdims=True)
        m_ref[r] = jnp.broadcast_to(m, m_ref.shape[1:])


def project_last(block, q, top, w, group=8):
    rows, cols, width = q.shape
    lanes = jnp.arange(width) // HEAD_DIM
    e = (lanes[:, None] == lanes[None, :]).astype(jnp.bfloat16)
    one = lambda c: pl.BlockSpec((group, c, width), lambda i: (i, 0, 0))
    shape = jax.ShapeDtypeStruct((rows, cols, width), jnp.bfloat16)
    return pl.pallas_call(
        project_last_kernel,
        grid=(rows // group,),
        out_shape=(shape, shape, jax.ShapeDtypeStruct((rows, 8, width), jnp.float32)),
        in_specs=[VMEM] * 2 + [one(cols), one(cols), one(8)],
        out_specs=(one(cols), one(cols), one(8)),
        compiler_params=PARAMS,
        cost_estimate=pl.CostEstimate(
            flops=10 * rows * cols * width * width,
            bytes_accessed=8 * rows * cols * width,
            transcendentals=0,
        ),
    )(w, e, block, q, top)


def attention_kernel(halves, me_ref, bias_a_ref, bias_b_ref, wo_ref, reach_ref, *refs):
    q_ref, g_ref, x_ref, ka_ref, va_ref, kb_ref, vb_ref = refs[:7]
    masks = refs[7 : 7 + halves]
    out_ref, flags, mrow, vs, b32, gated = refs[-6:]
    i = pl.program_id(0)
    group, cols, width = q_ref.shape
    _, outer, heads, sub, _ = bias_a_ref.shape
    lane = lax.broadcasted_iota(jnp.int32, (1, width), 1)
    me = me_ref[0]
    where = [lax.rem(me + s, halves) for s in (0, halves - 1, 1, 2)]
    step = cols // 128
    count = mrow.shape[1] // step

    @pl.when(i == 0)
    def _():
        top = jnp.zeros((sub, cols), jnp.float32)
        for s, w in enumerate(where):

            def put(t, top, s=s, w=w):
                for p, piece in enumerate((bias_a_ref, bias_b_ref)):
                    core = me_ref[1] if p == 0 else 1 - me_ref[1]
                    j = pl.ds(pl.multiple_of((2 * t + core) * sub, sub), sub)
                    for h in range(heads):
                        b = piece[w, t, h].astype(jnp.float32)
                        b32[h, j, s * cols : (s + 1) * cols] = b
                        top = jnp.maximum(top, jnp.abs(b))
                return top

            top = lax.fori_loop(0, outer, put, top)
        bound = jnp.max(reach_ref[...]) * 1.02 + jnp.max(top)
        flags[0] = (bound < SAFE).astype(jnp.int32)
        for s in range(halves):
            mrow[s] = masks[s][0, : mrow.shape[1], :].astype(jnp.float32)
        least = None
        seen = jnp.max(mrow[...], axis=0)
        for r in range(count):
            u = jnp.max(seen[r * step : (r + 1) * step], keepdims=True)
            least = u if least is None else jnp.minimum(least, u)
        flags[1] = (jnp.max(least) > 0.0).astype(jnp.int32)
        vs[:, :, width:] = jnp.ones((group, vs.shape[1], width), jnp.bfloat16)

    def mask_line(r):
        at = (i * group + r) * step
        return jnp.concatenate(
            [mrow[s, pl.ds(at + t, 1), :] for s in range(halves) for t in range(step)], axis=1
        )

    def finish(r, attended):
        gated[r] = (attended * g_ref[r].astype(jnp.float32)).astype(jnp.bfloat16)

    def attend(shift):
        def score(r, h):
            q = q_ref[r]
            on = jnp.broadcast_to(lane // (width // heads) == h, q.shape)
            qm = jnp.where(on, q, jnp.zeros_like(q))
            scores = jnp.concatenate([dot_nt(qm, ka_ref[r]), dot_nt(qm, kb_ref[r])], axis=1)
            return scores + b32[h] + jnp.where(mask_line(r) > 0.0, 0.0, NEG)

        order = [(r, h) for r in range(group) for h in range(heads)]
        ahead = [score(*order[t]) for t in range(AHEAD)]
        for t, (r, h) in enumerate(order):
            if t + AHEAD < len(order):
                ahead.append(score(*order[t + AHEAD]))
            scores = ahead.pop(0)
            if h == 0:
                vs[r, : va_ref.shape[1], :width] = va_ref[r]
                vs[r, va_ref.shape[1] :, :width] = vb_ref[r]
                num = jnp.zeros((cols, width), jnp.float32)
                den = jnp.ones((cols, width), jnp.float32)
            if shift:
                scores = scores - jnp.max(scores, axis=-1, keepdims=True)
            weights = jnp.exp2(scores).astype(jnp.bfloat16)
            both = dot_nn(weights, vs[r])
            on = lane // (width // heads) == h
            num = jnp.where(on, both[:, :width], num)
            den = jnp.where(on, both[:, width:], den)
            if h == heads - 1:
                finish(r, num / den)

    @pl.when(flags[0] > 0)
    def _():
        attend(False)

    @pl.when(flags[0] == 0)
    def _():
        attend(True)

    @pl.when(flags[1] == 0)
    def _():
        for r in range(group):
            used = jnp.max(mask_line(r), keepdims=True) > 0.0
            mean = jnp.mean(vs[r, :, :width].astype(jnp.float32), axis=0, keepdims=True)
            plain = mean * g_ref[r].astype(jnp.float32)
            gated[r] = jnp.where(used, gated[r].astype(jnp.float32), plain).astype(jnp.bfloat16)

    flat = (group * cols, width)
    out = dot_nn(gated[...].reshape(flat), wo_ref[...])
    out = x_ref[...].reshape(flat).astype(jnp.float32) + out
    out_ref[...] = out.astype(jnp.bfloat16).reshape(out_ref.shape)


def attention(me, bias, wo, reach, q, g, x, ka, va, kb, vb, blocks, chunk, filled, group=4):
    halves, _, heads, _, _ = bias[0].shape
    rows, cols, width = q.shape
    one = lambda c: pl.BlockSpec((group, c, width), lambda i: (i, 0, 0))
    last = pl.BlockSpec((1, cols, width), lambda i: (rows, 0, 0))
    na, nb = ka.shape[1], kb.shape[1]
    return pl.pallas_call(
        functools.partial(attention_kernel, halves),
        grid=(rows // group,),
        out_shape=jax.ShapeDtypeStruct((CHUNKS * rows, cols, width), jnp.bfloat16),
        in_specs=[SMEM, VMEM, VMEM, VMEM, VMEM]
        + [one(cols)] * 3
        + [one(na), one(na), one(nb), one(nb)]
        + [last] * halves
        + [pl.BlockSpec(memory_space=pl.ANY)] * len(filled),
        out_specs=pl.BlockSpec((group, cols, width), lambda i: (chunk * (rows // group) + i, 0, 0)),
        input_output_aliases={12 + halves: 0} if filled else {},
        scratch_shapes=[
            pltpu.SMEM((2,), jnp.int32),
            pltpu.VMEM((halves, rows * cols // 128, 128), jnp.float32),
            pltpu.VMEM((group, halves * cols, 2 * width), jnp.bfloat16),
            pltpu.VMEM((heads, cols, halves * cols), jnp.float32),
            pltpu.VMEM((group, cols, width), jnp.bfloat16),
        ],
        compiler_params=PARAMS,
        cost_estimate=pl.CostEstimate(
            flops=8 * rows * 4 * cols * halves * cols * width * 2,
            bytes_accessed=8 * rows * cols * width * halves,
            transcendentals=rows * 4 * cols * cols * halves,
        ),
    )(me, *bias, wo, reach, q, g, x, ka, va, kb, vb, *blocks, *filled)


def shards(sizes, pair, pair_mask, gains, w_tri, w_tri_out, w_att, w_bias, w_att_out):
    n_rows, halves = sizes
    rows, cols, width = pair.shape
    heads = w_bias.shape[1]
    lr = edges(pair, pair_mask, gains, w_tri)
    lr = lax.all_to_all(lr, AXES, split_axis=0, concat_axis=0, tiled=True)
    gates = gate(pair, gains, w_tri)
    prod = product(lr.reshape(n_rows, halves, 2, rows, cols))
    back = lax.all_to_all(
        prod.reshape(width, rows, cols), AXES, split_axis=0, concat_axis=0, tiled=True
    )
    wb = jnp.pad(w_bias.T, ((0, 8 - heads), (0, 0)))
    mask_flat = pair_mask.astype(jnp.bfloat16).reshape(rows * cols // width, width)
    up = [(y, (y + 1) % halves) for y in range(halves)]
    down = [(y, (y - 1) % halves) for y in range(halves)]
    after, blocks, bias = [], [], []
    for c in range(CHUNKS):
        x, own, b = tri_output(
            back, pair, gates, mask_flat, gains, gains[1][:, None], w_tri_out, wb, heads, c
        )
        prev = lax.ppermute(own, "half", up)
        next_ = lax.ppermute(own, "half", down)
        far = lax.ppermute(prev, "half", up) if c % 2 == 0 else lax.ppermute(next_, "half", down)
        after.append(x)
        blocks.append((own, prev, next_, far))
        bias.append(b)
    inner = n_rows // halves
    swap = [
        ((z * inner + k) * halves + y, (y * inner + k) * halves + z)
        for z in range(halves)
        for k in range(inner)
        for y in range(halves)
    ]
    bias = jnp.swapaxes(jnp.concatenate(bias, axis=0), 0, 1)
    bias = lax.ppermute(bias, AXES, swap)
    bias, near = lax.optimization_barrier((bias, blocks[0][1:3]))
    blocks[0] = (blocks[0][0], *near, blocks[0][3])
    half_rows = n_rows // 2
    bias = jnp.broadcast_to(bias[None], (half_rows,) + bias.shape)
    cores = [[2 * t + core for t in range(half_rows)] for core in range(2)]
    bias = lax.all_to_all(
        bias, "rows", split_axis=0, concat_axis=0, axis_index_groups=cores, tiled=True
    )
    other = lax.ppermute(bias, "rows", [(r, r ^ 1) for r in range(n_rows)])
    bias = [v.reshape(halves, inner // 2, heads, rows, cols) for v in (bias, other)]

    *bias, near = lax.optimization_barrier((*bias, blocks[1][2]))
    blocks[1] = (*blocks[1][:2], near, blocks[1][3])
    me = jnp.stack([lax.axis_index("half"), lax.axis_index("rows") & 1]).astype(jnp.int32)
    out = []
    for c, (own, prev, next_, far) in enumerate(blocks):
        if out:
            prev, far, out[0] = lax.optimization_barrier((prev, far, out[0]))
            blocks[c] = (own, prev, next_, far)
        q, g, ka, va, top = project((own, prev, next_), w_att)
        kb, vb, reach = project_last(far, q, top, w_att)
        out = [
            attention(
                me, bias, w_att_out, reach, q, g, after[c], ka, va, kb, vb, blocks[c], c, out
            )
        ]
    return out[0]


def solution(mesh):
    sizes = (mesh.shape["rows"], mesh.shape["half"])
    in_specs = (P("rows", "half", None), P("rows", "half"), P(), P(), P(), P(), P(), P())
    out_specs = P("rows", "half", None)
    return jax.shard_map(
        functools.partial(shards, sizes),
        mesh=mesh,
        in_specs=in_specs,
        out_specs=out_specs,
        check_vma=False,
    )
```

profile of v0, /device:TPU:100, one launch (start us, length us, event | category | flops | bytes accessed | tf_op | source)
XLA Modules:
  0.0 262.9 jit_solution(2953992142183599360)
XLA Ops:
  0.0 8.3 %shard_map.82 = bf16[128,2,32,256]{3,2,1,0:T(8,128)(2,1)} custom-call(bf16[32,256,128]{2,1,0:T(8,128)(2,1)} %pair_ref.7, s32[32,256]{1,0:T(8,128)} %mask_ref.1, f32[3,128]{1,0:T(4,128)} %gain_ref.7, bf16[128,640]{1,0:T(8,128)(2,1)} %w_ref.7), custom_call_target="tpu_custom_call" | custom-call | tf_op jit(solution)/shard_map/pallas_call | solution.py:84
  8.3 58.6 %all_to_all.15 = bf16[128,2,32,256]{3,2,1,0:T(8,128)(2,1)} all-to-all(bf16[128,2,32,256]{3,2,1,0:T(8,128)(2,1)} %shard_map.82), channel_id=1, replica_groups=mesh['rows'=32,'half'=4] {'rows','half'}, dimensions={0} | all-to-all | bytes 8388608 | tf_op jit(solution)/shard_map/all_to_all | solution.py:455
  66.9 6.1 %shard_map.83 = bf16[32,4,32,256]{3,2,1,0:T(8,128)(2,1)} custom-call(bf16[32,4,2,32,256]{4,3,2,1,0:T(8,128)(2,1)} %bitcast.11), custom_call_target="tpu_custom_call" | custom-call | tf_op jit(solution)/shard_map/pallas_call | solution.py:150
  73.0 9.1 %all-to-all-start.1 = ((bf16[128,32,256]{2,1,0:T(8,128)(2,1)}), bf16[128,32,256]{2,1,0:T(8,128)(2,1)}, u32[]{:S(2)}, u32[]{:S(2)}) async-start(bf16[128,32,256]{2,1,0:T(8,128)(2,1)} %bitcast.12), calls=%async_computation.1 | async-start | bytes 4194304 | tf_op jit(solution)/shard_map/all_to_all | solution.py:458
  82.1 0.7 slice_bitcast_fusion
  82.8 0.7 copy.10.gcol_ref
  83.6 0.6 reshape.44.mask_ref
  84.2 0.6 pad.4.wb_ref
  84.8 5.6 %shard_map.84.gate_ref = bf16[32,256,128]{2,1,0:T(8,128)(2,1)} custom-call(bf16[32,256,128]{2,1,0:T(8,128)(2,1)} %pair_ref.7, f32[3,128]{1,0:T(4,128)} %gain_ref.7, bf16[128,640]{1,0:T(8,128)(2,1)} %w_ref.7), custom_call_target="tpu_custom_call" | custom-call | flops 805306368 | bytes 4194304 | tf_op jit(solution)/shard_map/pallas_call | solution.py:110
  90.4 17.7 %all-to-all-done.1.prod_ref = bf16[128,32,256]{2,1,0:T(8,128)(2,1)} async-done(((bf16[128,32,256]{2,1,0:T(8,128)(2,1)}), bf16[128,32,256]{2,1,0:T(8,128)(2,1)}, u32[]{:S(2)}, u32[]{:S(2)}) %all-to-all-start.1) | async-done | bytes 2097184 | tf_op jit(solution)/shard_map/all_to_all | solution.py:458
  108.1 6.0 %shard_map.85 = (bf16[16,256,128]{2,1,0:T(8,128)(2,1)}, bf16[17,256,128]{2,1,0:T(8,128)(2,1)}, bf16[16,4,256]{2,1,0:T(4,128)(2,1)}) custom-call(bf16[128,32,256]{2,1,0:T(8,128)(2,1)} %all-to-all-done.1.prod_ref, bf16[32,256,128]{2,1,0:T(8,128)(2,1)} %pair_ref.7, bf16[32,256,128]{2,1,0:T(8,128)(2,1)} %shard_map.84.gate_ref, ...), custom_call_target="tpu_custom_call" | custom-call | tf_op jit(solution)/shard_map/pallas_call | solution.py:205
  114.0 0.6 collective-permute-start.1
  114.7 2.6 collective-permute-start.2
  117.3 5.9 %shard_map.86 = (bf16[16,256,128]{2,1,0:T(8,128)(2,1)}, bf16[17,256,128]{2,1,0:T(8,128)(2,1)}, bf16[16,4,256]{2,1,0:T(4,128)(2,1)}) custom-call(bf16[128,32,256]{2,1,0:T(8,128)(2,1)} %all-to-all-done.1.prod_ref, bf16[32,256,128]{2,1,0:T(8,128)(2,1)} %pair_ref.7, bf16[32,256,128]{2,1,0:T(8,128)(2,1)} %shard_map.84.gate_ref, ...), custom_call_target="tpu_custom_call" | custom-call | tf_op jit(solution)/shard_map/pallas_call | solution.py:205
  123.2 0.8 maximum_bitcast_fusion
  124.0 3.4 %collective-permute-start = (bf16[4,32,256]{2,0,1:T(4,128)(2,1)S(1)}, bf16[4,32,256]{2,0,1:T(4,128)(2,1)S(1)}, u32[]{:S(2)}, u32[]{:S(2)}) collective-permute-start(bf16[4,32,256]{2,0,1:T(4,128)(2,1)S(1)} %maximum_bitcast_fusion), channel_id=1, source_target_pairs={{0,0},{1,32},{2,64},{3,96},{4,4},{5,36},{6,68},{7,100},{8,8},{9,40... | collective-permute-start | bytes 196616 | tf_op jit(solution)/shard_map/ppermute | solution.py:484
  127.5 18.8 %collective-permute-done = bf16[4,32,256]{2,0,1:T(4,128)(2,1)S(1)} collective-permute-done((bf16[4,32,256]{2,0,1:T(4,128)(2,1)S(1)}, bf16[4,32,256]{2,0,1:T(4,128)(2,1)S(1)}, u32[]{:S(2)}, u32[]{:S(2)}) %collective-permute-start) | collective-permute-done | bytes 65568 | tf_op jit(solution)/shard_map/ppermute | solution.py:484
  146.3 1.2 broadcast_in_dim.2
  147.5 0.1 copy-done.4
  147.7 7.2 %all-to-all-start.2 = ((bf16[16,4,32,256]{3,2,1,0:T(8,128)(2,1)}), bf16[16,4,32,256]{3,2,1,0:T(8,128)(2,1)S(1)}, u32[]{:S(2)}, u32[]{:S(2)}) async-start(bf16[16,4,32,256]{3,2,1,0:T(8,128)(2,1)} %broadcast_in_dim.2), calls=%async_computation.2 | async-start | bytes 2097152 | tf_op jit(solution)/shard_map/all_to_all | solution.py:490
  154.9 2.1 collective-permute-start.4
  157.0 9.9 %all-to-all-done.2 = bf16[16,4,32,256]{3,2,1,0:T(8,128)(2,1)S(1)} async-done(((bf16[16,4,32,256]{3,2,1,0:T(8,128)(2,1)}), bf16[16,4,32,256]{3,2,1,0:T(8,128)(2,1)S(1)}, u32[]{:S(2)}, u32[]{:S(2)}) %all-to-all-start.2) | async-done | bytes 1048608 | tf_op jit(solution)/shard_map/all_to_all | solution.py:490
  166.9 0.7 pad_add_fusion.me_ref
  167.7 0.7 compare_convert_fusion.e_ref
  168.4 11.5 %collective-permute-done.4.refs_2_.refs_9_ = bf16[17,256,128]{2,1,0:T(8,128)(2,1)} collective-permute-done((bf16[17,256,128]{2,1,0:T(8,128)(2,1)}, bf16[17,256,128]{2,1,0:T(8,128)(2,1)}, u32[]{:S(2)}, u32[]{:S(2)}) %collective-permute-start.4) | collective-permute-done | bytes 1114144 | tf_op jit(solution)/shard_map/ppermute | solution.py:471
  179.9 3.6 %collective-permute-start.6 = (bf16[17,256,128]{2,1,0:T(8,128)(2,1)}, bf16[17,256,128]{2,1,0:T(8,128)(2,1)}, u32[]{:S(2)}, u32[]{:S(2)}) collective-permute-start(bf16[17,256,128]{2,1,0:T(8,128)(2,1)} %collective-permute-done.4.refs_2_.refs_9_), channel_id=1, source_target_pairs={{0,3},{1,0},{2,1},{3,2},{4,7},{5,4},{6,5},{7,6},{8,11},{9,8},{10,9... | collective-permute-start | bytes 3342344 | tf_op jit(solution)/shard_map/ppermute | solution.py:472
  183.5 5.9 %shard_map.87 = (bf16[16,256,128]{2,1,0:T(8,128)(2,1)}, bf16[16,256,128]{2,1,0:T(8,128)(2,1)}, bf16[16,768,128]{2,1,0:T(8,128)(2,1)}, bf16[16,768,128]{2,1,0:T(8,128)(2,1)}, f32[16,8,128]{2,1,0:T(8,128)}) custom-call(bf16[128,512]{1,0:T(8,128)(2,1)} %w_ref.11, bf16[17,256,128]{2,1,0:T(8,128)(2,1)} %get-tuple-element.38.refs_0_.refs_7_, ...), custom_call_target="tpu_custom_call" | custom-call | flops 1610612736 | bytes 12582912 | tf_op jit(solution)/shard_map/pallas_call | solution.py:262
  189.4 3.6 %shard_map.88 = (bf16[16,256,128]{2,1,0:T(8,128)(2,1)}, bf16[16,256,128]{2,1,0:T(8,128)(2,1)}, f32[16,8,128]{2,1,0:T(8,128)}) custom-call(bf16[128,512]{1,0:T(8,128)(2,1)} %w_ref.11, bf16[128,128]{1,0:T(8,128)(2,1)} %compare_convert_fusion.e_ref, bf16[17,256,128]{2,1,0:T(8,128)(2,1)} %collective-permute-done.7.x_ref.refs_10_, ...), custom_call_target="tpu_custom_call" | custom-call | flops 671088640 | bytes 4194304 | tf_op jit(solution)/shard_map/pallas_call | solution.py:301
  193.0 25.5 %shard_map.89.refs_11_ = bf16[32,256,128]{2,1,0:T(8,128)(2,1)} custom-call(s32[2]{0:T(128)} %pad_add_fusion.me_ref, bf16[4,4,4,32,256]{4,3,2,1,0:T(8,128)(2,1)} %bitcast.13, bf16[4,4,4,32,256]{4,3,2,1,0:T(8,128)(2,1)} %bitcast.8.bias_b_ref, bf16[128,128]{1,0:T(8,128)(2,1)} %wo_ref.7, f32[16,8,128]{2,1,0:T(8,128)} %get-tuple-element.47.reach_ref, ...), custom_call_target="tpu_custom_call" | custom-call | flops 34359738368 | bytes 16777216 | tf_op jit(solution)/shard_map/pallas_call | solution.py:423
  218.5 15.3 %shard_map.90 = (bf16[16,256,128]{2,1,0:T(8,128)(2,1)}, bf16[16,256,128]{2,1,0:T(8,128)(2,1)}, bf16[16,768,128]{2,1,0:T(8,128)(2,1)}, bf16[16,768,128]{2,1,0:T(8,128)(2,1)}, f32[16,8,128]{2,1,0:T(8,128)}) custom-call(bf16[128,512]{1,0:T(8,128)(2,1)} %w_ref.11, bf16[17,256,128]{2,1,0:T(8,128)(2,1)} %get-tuple-element.40.refs_0_.refs_7_, ...), custom_call_target="tpu_custom_call" | custom-call | flops 1610612736 | bytes 12582912 | tf_op jit(solution)/shard_map/pallas_call | solution.py:262
  233.8 3.6 %shard_map.91 = (bf16[16,256,128]{2,1,0:T(8,128)(2,1)}, bf16[16,256,128]{2,1,0:T(8,128)(2,1)}, f32[16,8,128]{2,1,0:T(8,128)}) custom-call(bf16[128,512]{1,0:T(8,128)(2,1)} %w_ref.11, bf16[128,128]{1,0:T(8,128)(2,1)} %compare_convert_fusion.e_ref, bf16[17,256,128]{2,1,0:T(8,128)(2,1)} %collective-permute-done.6.x_ref.refs_10_, ...), custom_call_target="tpu_custom_call" | custom-call | flops 671088640 | bytes 4194304 | tf_op jit(solution)/shard_map/pallas_call | solution.py:301
  237.4 25.3 %shard_map.92 = bf16[32,256,128]{2,1,0:T(8,128)(2,1)} custom-call(s32[2]{0:T(128)} %pad_add_fusion.me_ref, bf16[4,4,4,32,256]{4,3,2,1,0:T(8,128)(2,1)} %bitcast.14, bf16[4,4,4,32,256]{4,3,2,1,0:T(8,128)(2,1)} %bitcast.8.bias_b_ref, bf16[128,128]{1,0:T(8,128)(2,1)} %wo_ref.7, ...), custom_call_target="tpu_custom_call", output_to_operand_aliasing={{}: (16, {})} | custom-call | flops 34359738368 | bytes 16777216 | tf_op jit(solution)/shard_map/pallas_call | solution.py:423
  (21 shorter events, 0.1 us)
Async XLA Ops:
  73.0 9.1 %copy-start.1 = (s32[32,256]{1,0:T(8,128)S(1)}, s32[32,256]{1,0:T(8,128)}, u32[]{:S(2)}) copy-start(s32[32,256]{1,0:T(8,128)} %mask_ref.1) | copy-start | bytes 98308
  73.0 11.2 %copy-start.3 = (bf16[128,4]{0,1:T(4,128)(2,1)S(1)}, bf16[128,4]{0,1:T(4,128)(2,1)}, u32[]{:S(2)}) copy-start(bf16[128,4]{0,1:T(4,128)(2,1)} %param.14) | copy-start | bytes 3076
  73.0 35.1 %all-to-all-start.1 = ((bf16[128,32,256]{2,1,0:T(8,128)(2,1)}), bf16[128,32,256]{2,1,0:T(8,128)(2,1)}, u32[]{:S(2)}, u32[]{:S(2)}) async-start(bf16[128,32,256]{2,1,0:T(8,128)(2,1)} %bitcast.12), calls=%async_computation.1 | async-start | bytes 4194304 | tf_op jit(solution)/shard_map/all_to_all | solution.py:458
  114.0 9.2 %copy-start.2 = (bf16[16,4,256]{2,1,0:T(4,128)(2,1)S(1)}, bf16[16,4,256]{2,1,0:T(4,128)(2,1)}, u32[]{:S(2)}) copy-start(bf16[16,4,256]{2,1,0:T(4,128)(2,1)} %get-tuple-element.36) | copy-start | bytes 98308
  114.0 32.2 %collective-permute-start.1 = (bf16[17,256,128]{2,1,0:T(8,128)(2,1)}, bf16[17,256,128]{2,1,0:T(8,128)(2,1)S(1)}, u32[]{:S(2)}, u32[]{:S(2)}) collective-permute-start(bf16[17,256,128]{2,1,0:T(8,128)(2,1)} %get-tuple-element.38.refs_0_.refs_7_), channel_id=1, source_target_pairs={{0,1},{1,2},{2,3},{3,0},{4,5},{5,6},{6,7},{7,4},{8,9},{9,10},{10,1... | collective-permute-start | bytes 3342344 | tf_op jit(solution)/shard_map/ppermute | solution.py:470
  114.7 31.6 %collective-permute-start.2 = (bf16[17,256,128]{2,1,0:T(8,128)(2,1)}, bf16[17,256,128]{2,1,0:T(8,128)(2,1)}, u32[]{:S(2)}, u32[]{:S(2)}) collective-permute-start(bf16[17,256,128]{2,1,0:T(8,128)(2,1)} %get-tuple-element.38.refs_0_.refs_7_), channel_id=1, source_target_pairs={{0,3},{1,0},{2,1},{3,2},{4,7},{5,4},{6,5},{7,6},{8,11},{9,8},{10,9... | collective-permute-start | bytes 3342344 | tf_op jit(solution)/shard_map/ppermute | solution.py:471
  124.0 22.2 %collective-permute-start = (bf16[4,32,256]{2,0,1:T(4,128)(2,1)S(1)}, bf16[4,32,256]{2,0,1:T(4,128)(2,1)S(1)}, u32[]{:S(2)}, u32[]{:S(2)}) collective-permute-start(bf16[4,32,256]{2,0,1:T(4,128)(2,1)S(1)} %maximum_bitcast_fusion), channel_id=1, source_target_pairs={{0,0},{1,32},{2,64},{3,96},{4,4},{5,36},{6,68},{7,100},{8,8},{9,40... | collective-permute-start | bytes 196616 | tf_op jit(solution)/shard_map/ppermute | solution.py:484
  146.2 1.4 copy-start.4
  147.7 19.3 %all-to-all-start.2 = ((bf16[16,4,32,256]{3,2,1,0:T(8,128)(2,1)}), bf16[16,4,32,256]{3,2,1,0:T(8,128)(2,1)S(1)}, u32[]{:S(2)}, u32[]{:S(2)}) async-start(bf16[16,4,32,256]{3,2,1,0:T(8,128)(2,1)} %broadcast_in_dim.2), calls=%async_computation.2 | async-start | bytes 2097152 | tf_op jit(solution)/shard_map/all_to_all | solution.py:490
  154.9 25.0 %collective-permute-start.4 = (bf16[17,256,128]{2,1,0:T(8,128)(2,1)}, bf16[17,256,128]{2,1,0:T(8,128)(2,1)}, u32[]{:S(2)}, u32[]{:S(2)}) collective-permute-start(bf16[17,256,128]{2,1,0:T(8,128)(2,1)} %get-tuple-element.40.refs_0_.refs_7_), channel_id=1, source_target_pairs={{0,3},{1,0},{2,1},{3,2},{4,7},{5,4},{6,5},{7,6},{8,11},{9,8},{10,9... | collective-permute-start | bytes 3342344 | tf_op jit(solution)/shard_map/ppermute | solution.py:471
  157.0 32.4 %collective-permute-start.7 = (bf16[17,256,128]{2,1,0:T(8,128)(2,1)}, bf16[17,256,128]{2,1,0:T(8,128)(2,1)}, u32[]{:S(2)}, u32[]{:S(2)}) collective-permute-start(bf16[17,256,128]{2,1,0:T(8,128)(2,1)} %copy-done.4), channel_id=1, source_target_pairs={{0,1},{1,2},{2,3},{3,0},{4,5},{5,6},{6,7},{7,4},{8,9},{9,10},{10,1... | collective-permute-start | bytes 3342344 | tf_op jit(solution)/shard_map/ppermute | solution.py:472
  166.9 22.4 %copy-start = (bf16[16,4,32,256]{3,2,1,0:T(8,128)(2,1)}, bf16[16,4,32,256]{3,2,1,0:T(8,128)(2,1)S(1)}, u32[]{:S(2)}) copy-start(bf16[16,4,32,256]{3,2,1,0:T(8,128)(2,1)S(1)} %all-to-all-done.2) | copy-start | bytes 3145732
  166.9 26.1 %collective-permute-start.3 = (bf16[16,4,32,256]{3,2,1,0:T(8,128)(2,1)S(1)}, bf16[16,4,32,256]{3,2,1,0:T(8,128)(2,1)}, u32[]{:S(2)}, u32[]{:S(2)}) collective-permute-start(bf16[16,4,32,256]{3,2,1,0:T(8,128)(2,1)S(1)} %all-to-all-done.2), channel_id=1, source_target_pairs={{0,4},{4,0},{8,12},{12,8},{16,20},{20,16},{24,28},{28,24},{32,36},... | collective-permute-start | bytes 3145736 | tf_op jit(solution)/shard_map/ppermute | solution.py:493
  168.4 50.2 %collective-permute-start.5 = (bf16[17,256,128]{2,1,0:T(8,128)(2,1)}, bf16[17,256,128]{2,1,0:T(8,128)(2,1)}, u32[]{:S(2)}, u32[]{:S(2)}) collective-permute-start(bf16[17,256,128]{2,1,0:T(8,128)(2,1)} %get-tuple-element.40.refs_0_.refs_7_), channel_id=1, source_target_pairs={{0,1},{1,2},{2,3},{3,0},{4,5},{5,6},{6,7},{7,4},{8,9},{9,10},{10,1... | collective-permute-start | bytes 3342344 | tf_op jit(solution)/shard_map/ppermute | solution.py:470
  179.9 38.6 %collective-permute-start.6 = (bf16[17,256,128]{2,1,0:T(8,128)(2,1)}, bf16[17,256,128]{2,1,0:T(8,128)(2,1)}, u32[]{:S(2)}, u32[]{:S(2)}) collective-permute-start(bf16[17,256,128]{2,1,0:T(8,128)(2,1)} %collective-permute-done.4.refs_2_.refs_9_), channel_id=1, source_target_pairs={{0,3},{1,0},{2,1},{3,2},{4,7},{5,4},{6,5},{7,6},{8,11},{9,8},{10,9... | collective-permute-start | bytes 3342344 | tf_op jit(solution)/shard_map/ppermute | solution.py:472
where the time goes:
time: 268 us; the launch traced here: 263 us
  Pallas kernels  111 us (41%)
  blocking collectives  58.6 us (22%)
  waiting for transfers between devices  58 us (22%)
  starting transfers between devices  28.7 us (11%)
  local copies, waits for them, and re-layouts  4.04 us (2%)
    all_to_all x1, blocking collectives, shards(): lr = lax.all_to_all(lr, AXES, split_axis=0, concat_axis=0, tiled=True)  58.6 us
    pallas_call x2, Pallas kernels, attention(): pl.pallas_call(functools.partial(attention_kernel, halves), grid=(rows //...  50.8 us
    pallas_call x2, Pallas kernels, project(): pl.pallas_call(project_kernel, grid=(rows // group,), out_shape=(shape(co...  21.1 us
    ppermute x1, waiting for transfers between devices, shards(): bias = lax.ppermute(bias, AXES, swap)  18.8 us
    all_to_all x1, waiting for transfers between devices, shards(): lax.all_to_all(prod.reshape(width, rows, cols), AXES, split_axis=0, conca...  17.7 us
    pallas_call x2, Pallas kernels, tri_output(): pl.pallas_call(output_kernel, grid=(1,), out_shape=(jax.ShapeDtypeStruct(...  11.9 us
    ppermute x2, waiting for transfers between devices, shards(): next_ = lax.ppermute(own, 'half', down)  11.6 us
    all_to_all x1, waiting for transfers between devices, shards(): lax.all_to_all(bias, 'rows', split_axis=0, concat_axis=0, axis_index_grou...  9.92 us
  transfers between devices with their start and end apart: 10, of which 4 were waited for; matrix products, arithmetic and copies ran while one was open for 2% of the time, Pallas kernels for 18%

commit v1 on v0

--- a/solution.py
+++ b/solution.py
@@ -223,18 +223,23 @@
     )(prod, pair, gates, mask_flat, gains, gcol, wo, wb)
 
 
-def project_kernel(w_ref, *refs):
+def project_kernel(own, n, n_top, w_ref, *refs):
+    refs = list(refs)
+    take = lambda k: [refs.pop(0) for _ in range(k)]
+    xs, last = take(n), n_top > 0
+    (e_ref, q_in) = take(2) if last else (None, None)
+    tops_in = take(n_top)
+    q_ref, g_ref = take(2) if own else (None, None)
+    k_ref, v_ref, m_ref = refs
     width = w_ref.shape[0]
-    xs = refs[:-5]
-    q_ref, g_ref, k_ref, v_ref, m_ref = refs[-5:]
     group, cols, _ = xs[0].shape
-    scale = LOG2E * HEAD_DIM**-0.5
-    tops = [None] * group
+    tops = [functools.reduce(jnp.maximum, [t[r, 0:1, :] for t in tops_in]) if last else None for r in range(group)]
     for b, x_ref in enumerate(xs):
         a = x_ref[...].reshape(group * cols, width)
         at = slice(b * cols, (b + 1) * cols)
-        if b == 0:
+        if own:
             mixed = dot_nn(a, w_ref[...])
+            scale = LOG2E * HEAD_DIM**-0.5
             q_ref[...] = (mixed[:, :width] * scale).astype(jnp.bfloat16).reshape(q_ref.shape)
             g_ref[...] = sigmoid(mixed[:, 3 * width :]).astype(jnp.bfloat16).reshape(g_ref.shape)
             kv = mixed[:, width : 3 * width].astype(jnp.bfloat16)
@@ -244,78 +249,56 @@
         v_ref[:, at, :] = kv[:, width:].reshape(group, cols, width)
         for r in range(group):
             m = jnp.max(jnp.abs(kv[r * cols : (r + 1) * cols, :width]), axis=0, keepdims=True)
+            m = m.astype(jnp.float32)
             tops[r] = m if tops[r] is None else jnp.maximum(tops[r], m)
+    if last:
+        sized = [
+            (jnp.abs(q_in[r]).astype(jnp.float32) * tops[r]).astype(jnp.bfloat16)
+            for r in range(group)
+        ]
+        reach = dot_nn(jnp.concatenate(sized, axis=0), e_ref[...])
+        tops = [
+            jnp.max(reach[r * cols : (r + 1) * cols], axis=0, keepdims=True) for r in range(group)
+        ]
     for r in range(group):
-        m_ref[r] = jnp.broadcast_to(tops[r].astype(jnp.float32), m_ref.shape[1:])
+        m_ref[r] = jnp.broadcast_to(tops[r], m_ref.shape[1:])
 
 
 HEAD_DIM = 32
 AHEAD = 1
 
 
-def project(blocks, w, group=8):
+def project(blocks, w, own=False, q=None, tops=(), group=8):
     rows, cols, width = blocks[0].shape
     rows -= 1
     n = len(blocks)
     one = lambda c: pl.BlockSpec((group, c, width), lambda i: (i, 0, 0))
     shape = lambda c: jax.ShapeDtypeStruct((rows, c, width), jnp.bfloat16)
+    extra, specs = [], []
+    if tops:
+        lanes = jnp.arange(width) // HEAD_DIM
+        extra = [(lanes[:, None] == lanes[None, :]).astype(jnp.bfloat16), q, *tops]
+        specs = [VMEM, one(cols)] + [one(8)] * len(tops)
     return pl.pallas_call(
-        project_kernel,
+        functools.partial(project_kernel, own, n, len(tops)),
         grid=(rows // group,),
-        out_shape=(shape(cols), shape(cols), shape(n * cols), shape(n * cols), jax.ShapeDtypeStruct((rows, 8, width), jnp.float32)),
-        in_specs=[VMEM] + [one(cols)] * n,
-        out_specs=(one(cols), one(cols), one(n * cols), one(n * cols), one(8)),
+        out_shape=[shape(cols)] * (2 * own)
+        + [shape(n * cols), shape(n * cols), jax.ShapeDtypeStruct((rows, 8, width), jnp.float32)],
+        in_specs=[VMEM] + [one(cols)] * n + specs,
+        out_specs=[one(cols)] * (2 * own) + [one(n * cols), one(n * cols), one(8)],
         compiler_params=PARAMS,
         cost_estimate=pl.CostEstimate(
             flops=8 * n * rows * cols * width * width,
             bytes_accessed=8 * n * rows * cols * width,
             transcendentals=rows * cols * width,
         ),
-    )(w, *blocks)
-
-
-def project_last_kernel(w_ref, e_ref, x_ref, q_ref, top_ref, k_ref, v_ref, m_ref):
-    width = w_ref.shape[0]
-    group, cols, _ = x_ref.shape
-    a = x_ref[...].reshape(group * cols, width)
-    kv = dot_nn(a, w_ref[:, width : 3 * width]).astype(jnp.bfloat16)
-    k_ref[...] = kv[:, :width].reshape(k_ref.shape)
-    v_ref[...] = kv[:, width:].reshape(v_ref.shape)
-    sized = []
-    for r in range(group):
-        m = jnp.max(jnp.abs(kv[r * cols : (r + 1) * cols, :width]), axis=0, keepdims=True)
-        top = jnp.maximum(m.astype(jnp.float32), top_ref[r, 0:1, :])
-        sized.append((jnp.abs(q_ref[r]).astype(jnp.float32) * top).astype(jnp.bfloat16))
-    reach = dot_nn(jnp.concatenate(sized, axis=0), e_ref[...])
-    for r in range(group):
-        m = jnp.max(reach[r * cols : (r + 1) * cols], axis=0, keepdims=True)
-        m_ref[r] = jnp.broadcast_to(m, m_ref.shape[1:])
-
-
-def project_last(block, q, top, w, group=8):
-    rows, cols, width = q.shape
-    lanes = jnp.arange(width) // HEAD_DIM
-    e = (lanes[:, None] == lanes[None, :]).astype(jnp.bfloat16)
-    one = lambda c: pl.BlockSpec((group, c, width), lambda i: (i, 0, 0))
-    shape = jax.ShapeDtypeStruct((rows, cols, width), jnp.bfloat16)
-    return pl.pallas_call(
-        project_last_kernel,
-        grid=(rows // group,),
-        out_shape=(shape, shape, jax.ShapeDtypeStruct((rows, 8, width), jnp.float32)),
-        in_specs=[VMEM] * 2 + [one(cols), one(cols), one(8)],
-        out_specs=(one(cols), one(cols), one(8)),
-        compiler_params=PARAMS,
-        cost_estimate=pl.CostEstimate(
-            flops=10 * rows * cols * width * width,
-            bytes_accessed=8 * rows * cols * width,
-            transcendentals=0,
-        ),
-    )(w, e, block, q, top)
-
-
-def attention_kernel(halves, me_ref, bias_a_ref, bias_b_ref, wo_ref, reach_ref, *refs):
-    q_ref, g_ref, x_ref, ka_ref, va_ref, kb_ref, vb_ref = refs[:7]
-    masks = refs[7 : 7 + halves]
+    )(w, *blocks, *extra)
+
+
+def attention_kernel(halves, pieces, me_ref, bias_a_ref, bias_b_ref, wo_ref, reach_ref, *refs):
+    q_ref, g_ref, x_ref = refs[:3]
+    k_refs, v_refs = refs[3 : 3 + pieces], refs[3 + pieces : 3 + 2 * pieces]
+    masks = refs[3 + 2 * pieces : 3 + 2 * pieces + halves]
     out_ref, flags, mrow, vs, b32, gated = refs[-6:]
     i = pl.program_id(0)
     group, cols, width = q_ref.shape
@@ -368,7 +351,7 @@
             q = q_ref[r]
             on = jnp.broadcast_to(lane // (width // heads) == h, q.shape)
             qm = jnp.where(on, q, jnp.zeros_like(q))
-            scores = jnp.concatenate([dot_nt(qm, ka_ref[r]), dot_nt(qm, kb_ref[r])], axis=1)
+            scores = jnp.concatenate([dot_nt(qm, k[r]) for k in k_refs], axis=1)
             return scores + b32[h] + jnp.where(mask_line(r) > 0.0, 0.0, NEG)
 
         order = [(r, h) for r in range(group) for h in range(heads)]
@@ -378,8 +361,10 @@
                 ahead.append(score(*order[t + AHEAD]))
             scores = ahead.pop(0)
             if h == 0:
-                vs[r, : va_ref.shape[1], :width] = va_ref[r]
-                vs[r, va_ref.shape[1] :, :width] = vb_ref[r]
+                at = 0
+                for v in v_refs:
+                    vs[r, at : at + v.shape[1], :width] = v[r]
+                    at += v.shape[1]
                 num = jnp.zeros((cols, width), jnp.float32)
                 den = jnp.ones((cols, width), jnp.float32)
             if shift:
@@ -414,23 +399,23 @@
     out_ref[...] = out.astype(jnp.bfloat16).reshape(out_ref.shape)
 
 
-def attention(me, bias, wo, reach, q, g, x, ka, va, kb, vb, blocks, chunk, filled, group=4):
+def attention(me, bias, wo, reach, q, g, x, keys, values, blocks, chunk, filled, group=4):
     halves, _, heads, _, _ = bias[0].shape
     rows, cols, width = q.shape
     one = lambda c: pl.BlockSpec((group, c, width), lambda i: (i, 0, 0))
     last = pl.BlockSpec((1, cols, width), lambda i: (rows, 0, 0))
-    na, nb = ka.shape[1], kb.shape[1]
+    pieces = len(keys)
     return pl.pallas_call(
-        functools.partial(attention_kernel, halves),
+        functools.partial(attention_kernel, halves, pieces),
         grid=(rows // group,),
         out_shape=jax.ShapeDtypeStruct((CHUNKS * rows, cols, width), jnp.bfloat16),
         in_specs=[SMEM, VMEM, VMEM, VMEM, VMEM]
         + [one(cols)] * 3
-        + [one(na), one(na), one(nb), one(nb)]
+        + [one(k.shape[1]) for k in keys] * 2
         + [last] * halves
         + [pl.BlockSpec(memory_space=pl.ANY)] * len(filled),
         out_specs=pl.BlockSpec((group, cols, width), lambda i: (chunk * (rows // group) + i, 0, 0)),
-        input_output_aliases={12 + halves: 0} if filled else {},
+        input_output_aliases={8 + 2 * pieces + halves: 0} if filled else {},
         scratch_shapes=[
             pltpu.SMEM((2,), jnp.int32),
             pltpu.VMEM((halves, rows * cols // 128, 128), jnp.float32),
@@ -444,7 +429,7 @@
             bytes_accessed=8 * rows * cols * width * halves,
             transcendentals=rows * 4 * cols * cols * halves,
         ),
-    )(me, *bias, wo, reach, q, g, x, ka, va, kb, vb, *blocks, *filled)
+    )(me, *bias, wo, reach, q, g, x, *keys, *values, *blocks, *filled)
 
 
 def shards(sizes, pair, pair_mask, gains, w_tri, w_tri_out, w_att, w_bias, w_att_out):
@@ -490,25 +475,26 @@
     bias = lax.all_to_all(
         bias, "rows", split_axis=0, concat_axis=0, axis_index_groups=cores, tiled=True
     )
+    first = [project((b[0],), w_att, own=True) for b in blocks]
+    near = project(blocks[0][1:3], w_att)
+    bias, first, near = lax.optimization_barrier((bias, first, near))
     other = lax.ppermute(bias, "rows", [(r, r ^ 1) for r in range(n_rows)])
     bias = [v.reshape(halves, inner // 2, heads, rows, cols) for v in (bias, other)]
-
-    *bias, near = lax.optimization_barrier((*bias, blocks[1][2]))
-    blocks[1] = (*blocks[1][:2], near, blocks[1][3])
+    *bias, next_ = lax.optimization_barrier((*bias, blocks[1][2]))
+    blocks[1] = (*blocks[1][:2], next_, blocks[1][3])
+
     me = jnp.stack([lax.axis_index("half"), lax.axis_index("rows") & 1]).astype(jnp.int32)
-    out = []
-    for c, (own, prev, next_, far) in enumerate(blocks):
-        if out:
-            prev, far, out[0] = lax.optimization_barrier((prev, far, out[0]))
-            blocks[c] = (own, prev, next_, far)
-        q, g, ka, va, top = project((own, prev, next_), w_att)
-        kb, vb, reach = project_last(far, q, top, w_att)
-        out = [
-            attention(
-                me, bias, w_att_out, reach, q, g, after[c], ka, va, kb, vb, blocks[c], c, out
-            )
-        ]
-    return out[0]
+    q, g, k, v, top = first[0]
+    far = project((blocks[0][3],), w_att, q=q, tops=(top, near[2]))
+    out = attention(
+        me, bias, w_att_out, far[2], q, g, after[0], (k, near[0], far[0]), (v, near[1], far[1]), blocks[0], 0, []
+    )
+    rest, out = lax.optimization_barrier((blocks[1][1:], out))
+    q, g, k, v, top = first[1]
+    far = project(rest, w_att, q=q, tops=(top,))
+    return attention(
+        me, bias, w_att_out, far[2], q, g, after[1], (k, far[0]), (v, far[1]), (blocks[1][0], *rest), 1, [out]
+    )
 
 
 def solution(mesh):

time: 268 us -> 265 us (0.989)
  waiting for transfers between devices: 58 us -> 52.1 us
    all_to_all x1, waiting for transfers between devices: 9.92 us -> 0.01 us  [shards(): lax.all_to_all(bias, 'rows', split_axis=0, concat_axis=0, axis_index_grou...]
    ppermute x1, waiting for transfers between devices: 0.01 us -> 6.26 us  [shards(): lax.ppermute(prev, 'half', up)]
    pallas_call x6 -> x7, Pallas kernels: 79.2 us -> 80.4 us  [the longest x2 50.4 us: attention(): pl.pallas_call(functools.partial(attention_kernel, halves, pieces), grid=...]
  transfers between devices with their start and end apart: 10 -> 10, of which waited for: 4 -> 4; matrix products, arithmetic and copies ran while one was open for 2% -> 2% of each run, Pallas kernels for 18% -> 20%
where the time goes in v1:
time: 265 us; the launch traced here: 260 us
  Pallas kernels  112 us (42%)
  blocking collectives  58.6 us (22%)
  waiting for transfers between devices  52.1 us (20%)
  starting transfers between devices  29.8 us (11%)
  local copies, waits for them, and re-layouts  4.95 us (2%)
    all_to_all x1, blocking collectives, shards(): lr = lax.all_to_all(lr, AXES, split_axis=0, concat_axis=0, tiled=True)  58.6 us
    pallas_call x2, Pallas kernels, attention(): pl.pallas_call(functools.partial(attention_kernel, halves, pieces), grid=...  50.4 us
    pallas_call x5, Pallas kernels, project(): pl.pallas_call(functools.partial(project_kernel, own, n, len(tops)), grid...  30 us
    ppermute x1, waiting for transfers between devices, shards(): bias = lax.ppermute(bias, AXES, swap)  18.7 us
    all_to_all x1, waiting for transfers between devices, shards(): lax.all_to_all(prod.reshape(width, rows, cols), AXES, split_axis=0, conca...  17.7 us
    pallas_call x2, Pallas kernels, tri_output(): pl.pallas_call(output_kernel, grid=(1,), out_shape=(jax.ShapeDtypeStruct(...  12 us
    ppermute x2, waiting for transfers between devices, shards(): next_ = lax.ppermute(own, 'half', down)  9.41 us
    all_to_all x1, starting transfers between devices, shards(): lax.all_to_all(prod.reshape(width, rows, cols), AXES, split_axis=0, conca...  9.13 us
  transfers between devices with their start and end apart: 10, of which 4 were waited for; matrix products, arithmetic and copies ran while one was open for 2% of the time, Pallas kernels for 20%

profile of v1, /device:TPU:100, one launch (start us, length us, event | category | flops | bytes accessed | tf_op | source)
XLA Modules:
  0.0 260.3 jit_solution(8483212263678066385)
XLA Ops:
  0.0 8.3 %shard_map.82 = bf16[128,2,32,256]{3,2,1,0:T(8,128)(2,1)} custom-call(bf16[32,256,128]{2,1,0:T(8,128)(2,1)} %pair_ref.7, s32[32,256]{1,0:T(8,128)} %mask_ref.1, f32[3,128]{1,0:T(4,128)} %gain_ref.7, bf16[128,640]{1,0:T(8,128)(2,1)} %w_ref.8), custom_call_target="tpu_custom_call" | custom-call | tf_op jit(solution)/shard_map/pallas_call | solution.py:84
  8.3 58.6 %all_to_all.15 = bf16[128,2,32,256]{3,2,1,0:T(8,128)(2,1)} all-to-all(bf16[128,2,32,256]{3,2,1,0:T(8,128)(2,1)} %shard_map.82), channel_id=1, replica_groups=mesh['rows'=32,'half'=4] {'rows','half'}, dimensions={0} | all-to-all | bytes 8388608 | tf_op jit(solution)/shard_map/all_to_all | solution.py:440
  66.9 6.1 %shard_map.83 = bf16[32,4,32,256]{3,2,1,0:T(8,128)(2,1)} custom-call(bf16[32,4,2,32,256]{4,3,2,1,0:T(8,128)(2,1)} %bitcast.11), custom_call_target="tpu_custom_call" | custom-call | tf_op jit(solution)/shard_map/pallas_call | solution.py:150
  73.0 9.1 %all-to-all-start.1 = ((bf16[128,32,256]{2,1,0:T(8,128)(2,1)}), bf16[128,32,256]{2,1,0:T(8,128)(2,1)}, u32[]{:S(2)}, u32[]{:S(2)}) async-start(bf16[128,32,256]{2,1,0:T(8,128)(2,1)} %bitcast.12), calls=%async_computation.1 | async-start | bytes 4194304 | tf_op jit(solution)/shard_map/all_to_all | solution.py:443
  82.1 0.7 slice_bitcast_fusion
  82.8 0.7 copy.10.gcol_ref
  83.5 0.6 reshape.44.mask_ref
  84.2 0.6 pad.4.wb_ref
  84.8 5.6 %shard_map.84.gate_ref = bf16[32,256,128]{2,1,0:T(8,128)(2,1)} custom-call(bf16[32,256,128]{2,1,0:T(8,128)(2,1)} %pair_ref.7, f32[3,128]{1,0:T(4,128)} %gain_ref.7, bf16[128,640]{1,0:T(8,128)(2,1)} %w_ref.8), custom_call_target="tpu_custom_call" | custom-call | flops 805306368 | bytes 4194304 | tf_op jit(solution)/shard_map/pallas_call | solution.py:110
  90.4 17.7 %all-to-all-done.1.prod_ref = bf16[128,32,256]{2,1,0:T(8,128)(2,1)} async-done(((bf16[128,32,256]{2,1,0:T(8,128)(2,1)}), bf16[128,32,256]{2,1,0:T(8,128)(2,1)}, u32[]{:S(2)}, u32[]{:S(2)}) %all-to-all-start.1) | async-done | bytes 2097184 | tf_op jit(solution)/shard_map/all_to_all | solution.py:443
  108.1 6.0 %shard_map.85 = (bf16[16,256,128]{2,1,0:T(8,128)(2,1)}, bf16[17,256,128]{2,1,0:T(8,128)(2,1)}, bf16[16,4,256]{2,1,0:T(4,128)(2,1)}) custom-call(bf16[128,32,256]{2,1,0:T(8,128)(2,1)} %all-to-all-done.1.prod_ref, bf16[32,256,128]{2,1,0:T(8,128)(2,1)} %pair_ref.7, bf16[32,256,128]{2,1,0:T(8,128)(2,1)} %shard_map.84.gate_ref, ...), custom_call_target="tpu_custom_call" | custom-call | tf_op jit(solution)/shard_map/pallas_call | solution.py:205
  114.1 0.6 collective-permute-start.1
  114.8 2.6 collective-permute-start.2
  117.4 6.0 %shard_map.86 = (bf16[16,256,128]{2,1,0:T(8,128)(2,1)}, bf16[17,256,128]{2,1,0:T(8,128)(2,1)}, bf16[16,4,256]{2,1,0:T(4,128)(2,1)}) custom-call(bf16[128,32,256]{2,1,0:T(8,128)(2,1)} %all-to-all-done.1.prod_ref, bf16[32,256,128]{2,1,0:T(8,128)(2,1)} %pair_ref.7, bf16[32,256,128]{2,1,0:T(8,128)(2,1)} %shard_map.84.gate_ref, ...), custom_call_target="tpu_custom_call" | custom-call | tf_op jit(solution)/shard_map/pallas_call | solution.py:205
  123.3 0.8 maximum_bitcast_fusion
  124.1 3.4 %collective-permute-start = (bf16[4,32,256]{2,0,1:T(4,128)(2,1)S(1)}, bf16[4,32,256]{2,0,1:T(4,128)(2,1)S(1)}, u32[]{:S(2)}, u32[]{:S(2)}) collective-permute-start(bf16[4,32,256]{2,0,1:T(4,128)(2,1)S(1)} %maximum_bitcast_fusion), channel_id=1, source_target_pairs={{0,0},{1,32},{2,64},{3,96},{4,4},{5,36},{6,68},{7,100},{8,8},{9,40... | collective-permute-start | bytes 196616 | tf_op jit(solution)/shard_map/ppermute | solution.py:469
  127.6 18.7 %collective-permute-done = bf16[4,32,256]{2,0,1:T(4,128)(2,1)S(1)} collective-permute-done((bf16[4,32,256]{2,0,1:T(4,128)(2,1)S(1)}, bf16[4,32,256]{2,0,1:T(4,128)(2,1)S(1)}, u32[]{:S(2)}, u32[]{:S(2)}) %collective-permute-start) | collective-permute-done | bytes 65568 | tf_op jit(solution)/shard_map/ppermute | solution.py:469
  146.3 1.2 broadcast_in_dim.2
  147.5 7.2 %all-to-all-start.2 = ((bf16[16,4,32,256]{3,2,1,0:T(8,128)(2,1)}), bf16[16,4,32,256]{3,2,1,0:T(8,128)(2,1)}, u32[]{:S(2)}, u32[]{:S(2)}) async-start(bf16[16,4,32,256]{3,2,1,0:T(8,128)(2,1)} %broadcast_in_dim.2), calls=%async_computation.2 | async-start | bytes 2097152 | tf_op jit(solution)/shard_map/all_to_all | solution.py:475
  154.8 2.8 %collective-permute-start.4 = (bf16[17,256,128]{2,1,0:T(8,128)(2,1)}, bf16[17,256,128]{2,1,0:T(8,128)(2,1)}, u32[]{:S(2)}, u32[]{:S(2)}) collective-permute-start(bf16[17,256,128]{2,1,0:T(8,128)(2,1)} %get-tuple-element.63.refs_0_.refs_7_), channel_id=1, source_target_pairs={{0,3},{1,0},{2,1},{3,2},{4,7},{5,4},{6,5},{7,6},{8,11},{9,8},{10,9... | collective-permute-start | bytes 3342344 | tf_op jit(solution)/shard_map/ppermute | solution.py:456
  157.5 3.8 %shard_map.87 = (bf16[16,256,128]{2,1,0:T(8,128)(2,1)}, bf16[16,256,128]{2,1,0:T(8,128)(2,1)}, bf16[16,256,128]{2,1,0:T(8,128)(2,1)}, bf16[16,256,128]{2,1,0:T(8,128)(2,1)}, f32[16,8,128]{2,1,0:T(8,128)}) custom-call(bf16[128,512]{1,0:T(8,128)(2,1)} %w_ref.13, bf16[17,256,128]{2,1,0:T(8,128)(2,1)} %get-tuple-element.56.refs_0_.refs_9_), custom_call_target="tpu_custom_call" | custom-call | flops 536870912 | bytes 4194304 | tf_op jit(solution)/shard_map/pallas_call | solution.py:282
  161.3 3.9 %shard_map.88 = (bf16[16,256,128]{2,1,0:T(8,128)(2,1)}, bf16[16,256,128]{2,1,0:T(8,128)(2,1)}, bf16[16,256,128]{2,1,0:T(8,128)(2,1)}, bf16[16,256,128]{2,1,0:T(8,128)(2,1)}, f32[16,8,128]{2,1,0:T(8,128)}) custom-call(bf16[128,512]{1,0:T(8,128)(2,1)} %w_ref.13, bf16[17,256,128]{2,1,0:T(8,128)(2,1)} %get-tuple-element.63.refs_0_.refs_7_), custom_call_target="tpu_custom_call" | custom-call | flops 536870912 | bytes 4194304 | tf_op jit(solution)/shard_map/pallas_call | solution.py:282
  165.3 4.0 %shard_map.89 = (bf16[16,512,128]{2,1,0:T(8,128)(2,1)}, bf16[16,512,128]{2,1,0:T(8,128)(2,1)}, f32[16,8,128]{2,1,0:T(8,128)}) custom-call(bf16[128,512]{1,0:T(8,128)(2,1)} %w_ref.13, bf16[17,256,128]{2,1,0:T(8,128)(2,1)} %copy-done.4, bf16[17,256,128]{2,1,0:T(8,128)(2,1)} %collective-permute-done.2.refs_1_.refs_11_), custom_call_target="tpu_custom_call" | custom-call | flops 1073741824 | bytes 8388608 | tf_op jit(solution)/shard_map/pallas_call | solution.py:282
  170.2 0.7 compare_convert_fusion.refs_1_.refs_3_
  170.9 9.4 %collective-permute-done.4.refs_1_.refs_9_ = bf16[17,256,128]{2,1,0:T(8,128)(2,1)} collective-permute-done((bf16[17,256,128]{2,1,0:T(8,128)(2,1)}, bf16[17,256,128]{2,1,0:T(8,128)(2,1)}, u32[]{:S(2)}, u32[]{:S(2)}) %collective-permute-start.4) | collective-permute-done | bytes 1114144 | tf_op jit(solution)/shard_map/ppermute | solution.py:456
  180.3 3.7 %collective-permute-start.6 = (bf16[17,256,128]{2,1,0:T(8,128)(2,1)}, bf16[17,256,128]{2,1,0:T(8,128)(2,1)}, u32[]{:S(2)}, u32[]{:S(2)}) collective-permute-start(bf16[17,256,128]{2,1,0:T(8,128)(2,1)} %collective-permute-done.4.refs_1_.refs_9_), channel_id=1, source_target_pairs={{0,3},{1,0},{2,1},{3,2},{4,7},{5,4},{6,5},{7,6},{8,11},{9,8},{10,9... | collective-permute-start | bytes 3342344 | tf_op jit(solution)/shard_map/ppermute | solution.py:457
  184.0 6.3 %collective-permute-done.7.refs_0_.refs_12_ = bf16[17,256,128]{2,1,0:T(8,128)(2,1)S(1)} collective-permute-done((bf16[17,256,128]{2,1,0:T(8,128)(2,1)}, bf16[17,256,128]{2,1,0:T(8,128)(2,1)S(1)}, u32[]{:S(2)}, u32[]{:S(2)}) %collective-permute-start.7) | collective-permute-done | bytes 1114144 | tf_op jit(solution)/shard_map/ppermute | solution.py:457
  190.3 1.1 copy-done
  191.3 3.6 %shard_map.90 = (bf16[16,256,128]{2,1,0:T(8,128)(2,1)}, bf16[16,256,128]{2,1,0:T(8,128)(2,1)}, f32[16,8,128]{2,1,0:T(8,128)}) custom-call(bf16[128,512]{1,0:T(8,128)(2,1)} %w_ref.13, bf16[17,256,128]{2,1,0:T(8,128)(2,1)} %copy-done, bf16[128,128]{1,0:T(8,128)(2,1)} %compare_convert_fusion.refs_1_.refs_3_, ...), custom_call_target="tpu_custom_call" | custom-call | flops 536870912 | bytes 4194304 | tf_op jit(solution)/shard_map/pallas_call | solution.py:282
  195.0 25.3 %shard_map.91.refs_11_ = bf16[32,256,128]{2,1,0:T(8,128)(2,1)} custom-call(s32[2]{0:T(128)} %pad_add_fusion.me_ref, bf16[4,4,4,32,256]{4,3,2,1,0:T(8,128)(2,1)} %bitcast.7.bias_a_ref, bf16[4,4,4,32,256]{4,3,2,1,0:T(8,128)(2,1)} %bitcast.8.bias_b_ref, bf16[128,128]{1,0:T(8,128)(2,1)} %wo_ref.7, f32[16,8,128]{2,1,0:T(8,128)} %get-tuple-element.81.reach_ref, ...), custom_call_target="tpu_custom_call" | custom-call | flops 34359738368 | bytes 16777216 | tf_op jit(solution)/shard_map/pallas_call | solution.py:408
  220.3 14.7 %shard_map.92 = (bf16[16,768,128]{2,1,0:T(8,128)(2,1)}, bf16[16,768,128]{2,1,0:T(8,128)(2,1)}, f32[16,8,128]{2,1,0:T(8,128)}) custom-call(bf16[128,512]{1,0:T(8,128)(2,1)} %w_ref.13, bf16[17,256,128]{2,1,0:T(8,128)(2,1)} %collective-permute-done.5.refs_0_.refs_8_, bf16[17,256,128]{2,1,0:T(8,128)(2,1)} %collective-permute-done.4.refs_1_.refs_9_, ...), custom_call_target="tpu_custom_call" | custom-call | flops 1610612736 | bytes 12582912 | tf_op jit(solution)/shard_map/pallas_call | solution.py:282
  235.0 25.1 %shard_map.93 = bf16[32,256,128]{2,1,0:T(8,128)(2,1)} custom-call(s32[2]{0:T(128)} %pad_add_fusion.me_ref, bf16[4,4,4,32,256]{4,3,2,1,0:T(8,128)(2,1)} %bitcast.7.bias_a_ref, bf16[4,4,4,32,256]{4,3,2,1,0:T(8,128)(2,1)} %bitcast.8.bias_b_ref, bf16[128,128]{1,0:T(8,128)(2,1)} %wo_ref.7, ...), custom_call_target="tpu_custom_call", output_to_operand_aliasing={{}: (16, {})} | custom-call | flops 34359738368 | bytes 16777216 | tf_op jit(solution)/shard_map/pallas_call | solution.py:408
  (22 shorter events, 1.0 us)
Async XLA Ops:
  73.0 9.1 %copy-start.1 = (s32[32,256]{1,0:T(8,128)S(1)}, s32[32,256]{1,0:T(8,128)}, u32[]{:S(2)}) copy-start(s32[32,256]{1,0:T(8,128)} %mask_ref.1) | copy-start | bytes 98308
  73.0 11.2 %copy-start.3 = (bf16[128,4]{0,1:T(4,128)(2,1)S(1)}, bf16[128,4]{0,1:T(4,128)(2,1)}, u32[]{:S(2)}) copy-start(bf16[128,4]{0,1:T(4,128)(2,1)} %param.14) | copy-start | bytes 3076
  73.0 35.1 %all-to-all-start.1 = ((bf16[128,32,256]{2,1,0:T(8,128)(2,1)}), bf16[128,32,256]{2,1,0:T(8,128)(2,1)}, u32[]{:S(2)}, u32[]{:S(2)}) async-start(bf16[128,32,256]{2,1,0:T(8,128)(2,1)} %bitcast.12), calls=%async_computation.1 | async-start | bytes 4194304 | tf_op jit(solution)/shard_map/all_to_all | solution.py:443
  114.1 9.2 %copy-start.2 = (bf16[16,4,256]{2,1,0:T(4,128)(2,1)S(1)}, bf16[16,4,256]{2,1,0:T(4,128)(2,1)}, u32[]{:S(2)}) copy-start(bf16[16,4,256]{2,1,0:T(4,128)(2,1)} %get-tuple-element.54) | copy-start | bytes 98308
  114.1 32.2 %collective-permute-start.1 = (bf16[17,256,128]{2,1,0:T(8,128)(2,1)}, bf16[17,256,128]{2,1,0:T(8,128)(2,1)S(1)}, u32[]{:S(2)}, u32[]{:S(2)}) collective-permute-start(bf16[17,256,128]{2,1,0:T(8,128)(2,1)} %get-tuple-element.56.refs_0_.refs_9_), channel_id=1, source_target_pairs={{0,1},{1,2},{2,3},{3,0},{4,5},{5,6},{6,7},{7,4},{8,9},{9,10},{10,1... | collective-permute-start | bytes 3342344 | tf_op jit(solution)/shard_map/ppermute | solution.py:455
  114.8 31.6 %collective-permute-start.2 = (bf16[17,256,128]{2,1,0:T(8,128)(2,1)}, bf16[17,256,128]{2,1,0:T(8,128)(2,1)}, u32[]{:S(2)}, u32[]{:S(2)}) collective-permute-start(bf16[17,256,128]{2,1,0:T(8,128)(2,1)} %get-tuple-element.56.refs_0_.refs_9_), channel_id=1, source_target_pairs={{0,3},{1,0},{2,1},{3,2},{4,7},{5,4},{6,5},{7,6},{8,11},{9,8},{10,9... | collective-permute-start | bytes 3342344 | tf_op jit(solution)/shard_map/ppermute | solution.py:456
  124.1 22.2 %collective-permute-start = (bf16[4,32,256]{2,0,1:T(4,128)(2,1)S(1)}, bf16[4,32,256]{2,0,1:T(4,128)(2,1)S(1)}, u32[]{:S(2)}, u32[]{:S(2)}) collective-permute-start(bf16[4,32,256]{2,0,1:T(4,128)(2,1)S(1)} %maximum_bitcast_fusion), channel_id=1, source_target_pairs={{0,0},{1,32},{2,64},{3,96},{4,4},{5,36},{6,68},{7,100},{8,8},{9,40... | collective-permute-start | bytes 196616 | tf_op jit(solution)/shard_map/ppermute | solution.py:469
  146.3 11.2 %copy-start.4 = (bf16[17,256,128]{2,1,0:T(8,128)(2,1)}, bf16[17,256,128]{2,1,0:T(8,128)(2,1)S(1)}, u32[]{:S(2)}) copy-start(bf16[17,256,128]{2,1,0:T(8,128)(2,1)S(1)} %collective-permute-done.1.refs_0_.refs_10_) | copy-start | bytes 3342340
  147.5 21.7 %all-to-all-start.2 = ((bf16[16,4,32,256]{3,2,1,0:T(8,128)(2,1)}), bf16[16,4,32,256]{3,2,1,0:T(8,128)(2,1)}, u32[]{:S(2)}, u32[]{:S(2)}) async-start(bf16[16,4,32,256]{3,2,1,0:T(8,128)(2,1)} %broadcast_in_dim.2), calls=%async_computation.2 | async-start | bytes 2097152 | tf_op jit(solution)/shard_map/all_to_all | solution.py:475
  154.8 25.5 %collective-permute-start.4 = (bf16[17,256,128]{2,1,0:T(8,128)(2,1)}, bf16[17,256,128]{2,1,0:T(8,128)(2,1)}, u32[]{:S(2)}, u32[]{:S(2)}) collective-permute-start(bf16[17,256,128]{2,1,0:T(8,128)(2,1)} %get-tuple-element.63.refs_0_.refs_7_), channel_id=1, source_target_pairs={{0,3},{1,0},{2,1},{3,2},{4,7},{5,4},{6,5},{7,6},{8,11},{9,8},{10,9... | collective-permute-start | bytes 3342344 | tf_op jit(solution)/shard_map/ppermute | solution.py:456
  161.3 28.9 %collective-permute-start.7 = (bf16[17,256,128]{2,1,0:T(8,128)(2,1)}, bf16[17,256,128]{2,1,0:T(8,128)(2,1)S(1)}, u32[]{:S(2)}, u32[]{:S(2)}) collective-permute-start(bf16[17,256,128]{2,1,0:T(8,128)(2,1)} %copy-done.4), channel_id=1, source_target_pairs={{0,1},{1,2},{2,3},{3,0},{4,5},{5,6},{6,7},{7,4},{8,9},{9,10},{10,1... | collective-permute-start | bytes 3342344 | tf_op jit(solution)/shard_map/ppermute | solution.py:457
  169.2 25.7 %collective-permute-start.3 = (bf16[16,4,32,256]{3,2,1,0:T(8,128)(2,1)}, bf16[16,4,32,256]{3,2,1,0:T(8,128)(2,1)}, u32[]{:S(2)}, u32[]{:S(2)}) collective-permute-start(bf16[16,4,32,256]{3,2,1,0:T(8,128)(2,1)} %all-to-all-done.2), channel_id=1, source_target_pairs={{0,4},{4,0},{8,12},{12,8},{16,20},{20,16},{24,28},{28,24},{32,36},... | collective-permute-start | bytes 3145736 | tf_op jit(solution)/shard_map/ppermute | solution.py:481
  170.9 49.4 %collective-permute-start.5 = (bf16[17,256,128]{2,1,0:T(8,128)(2,1)}, bf16[17,256,128]{2,1,0:T(8,128)(2,1)}, u32[]{:S(2)}, u32[]{:S(2)}) collective-permute-start(bf16[17,256,128]{2,1,0:T(8,128)(2,1)} %get-tuple-element.63.refs_0_.refs_7_), channel_id=1, source_target_pairs={{0,1},{1,2},{2,3},{3,0},{4,5},{5,6},{6,7},{7,4},{8,9},{9,10},{10,1... | collective-permute-start | bytes 3342344 | tf_op jit(solution)/shard_map/ppermute | solution.py:455
  180.3 40.0 %collective-permute-start.6 = (bf16[17,256,128]{2,1,0:T(8,128)(2,1)}, bf16[17,256,128]{2,1,0:T(8,128)(2,1)}, u32[]{:S(2)}, u32[]{:S(2)}) collective-permute-start(bf16[17,256,128]{2,1,0:T(8,128)(2,1)} %collective-permute-done.4.refs_1_.refs_9_), channel_id=1, source_target_pairs={{0,3},{1,0},{2,1},{3,2},{4,7},{5,4},{6,5},{7,6},{8,11},{9,8},{10,9... | collective-permute-start | bytes 3342344 | tf_op jit(solution)/shard_map/ppermute | solution.py:457
  190.3 1.1 copy-start

commit v2 on v1

--- a/solution.py
+++ b/solution.py
@@ -467,7 +467,8 @@
     ]
     bias = jnp.swapaxes(jnp.concatenate(bias, axis=0), 0, 1)
     bias = lax.ppermute(bias, AXES, swap)
-    bias, near = lax.optimization_barrier((bias, blocks[0][1:3]))
+    first = [project((b[0],), w_att, own=True) for b in blocks]
+    bias, first, near = lax.optimization_barrier((bias, first, blocks[0][1:3]))
     blocks[0] = (blocks[0][0], *near, blocks[0][3])
     half_rows = n_rows // 2
     bias = jnp.broadcast_to(bias[None], (half_rows,) + bias.shape)
@@ -475,9 +476,8 @@
     bias = lax.all_to_all(
         bias, "rows", split_axis=0, concat_axis=0, axis_index_groups=cores, tiled=True
     )
-    first = [project((b[0],), w_att, own=True) for b in blocks]
     near = project(blocks[0][1:3], w_att)
-    bias, first, near = lax.optimization_barrier((bias, first, near))
+    bias, near = lax.optimization_barrier((bias, near))
     other = lax.ppermute(bias, "rows", [(r, r ^ 1) for r in range(n_rows)])
     bias = [v.reshape(halves, inner // 2, heads, rows, cols) for v in (bias, other)]
     *bias, next_ = lax.optimization_barrier((*bias, blocks[1][2]))

time: 265 us -> 261 us (0.985)
  waiting for transfers between devices: 52.1 us -> 48.5 us
    ppermute x1, waiting for transfers between devices: 18.7 us -> 11.1 us  [shards(): bias = lax.ppermute(bias, AXES, swap)]
    all_to_all x1, waiting for transfers between devices: 0.01 us -> 5.35 us  [shards(): lax.all_to_all(bias, 'rows', split_axis=0, concat_axis=0, axis_index_grou...]
    ppermute x1, waiting for transfers between devices: 6.26 us -> 2.45 us  [shards(): lax.ppermute(prev, 'half', up)]
  transfers between devices with their start and end apart: 10 -> 10, of which waited for: 4 -> 5; matrix products, arithmetic and copies ran while one was open for 2% -> 2% of each run, Pallas kernels for 20% -> 20%
where the time goes in v2:
time: 261 us; the launch traced here: 256 us
  Pallas kernels  112 us (43%)
  blocking collectives  58.6 us (22%)
  waiting for transfers between devices  48.5 us (19%)
  starting transfers between devices  29.8 us (11%)
  local copies, waits for them, and re-layouts  4.94 us (2%)
    all_to_all x1, blocking collectives, shards(): lr = lax.all_to_all(lr, AXES, split_axis=0, concat_axis=0, tiled=True)  58.6 us
    pallas_call x2, Pallas kernels, attention(): pl.pallas_call(functools.partial(attention_kernel, halves, pieces), grid=...  50.4 us
    pallas_call x5, Pallas kernels, project(): pl.pallas_call(functools.partial(project_kernel, own, n, len(tops)), grid...  29.9 us
    all_to_all x1, waiting for transfers between devices, shards(): lax.all_to_all(prod.reshape(width, rows, cols), AXES, split_axis=0, conca...  17.7 us
    pallas_call x2, Pallas kernels, tri_output(): pl.pallas_call(output_kernel, grid=(1,), out_shape=(jax.ShapeDtypeStruct(...  12 us
    ppermute x2, waiting for transfers between devices, shards(): next_ = lax.ppermute(own, 'half', down)  11.9 us
    ppermute x1, waiting for transfers between devices, shards(): bias = lax.ppermute(bias, AXES, swap)  11.1 us
    all_to_all x1, starting transfers between devices, shards(): lax.all_to_all(prod.reshape(width, rows, cols), AXES, split_axis=0, conca...  9.13 us
  transfers between devices with their start and end apart: 10, of which 5 were waited for; matrix products, arithmetic and copies ran while one was open for 2% of the time, Pallas kernels for 20%

profile of v2, /device:TPU:100, one launch (start us, length us, event | category | flops | bytes accessed | tf_op | source)
XLA Modules:
  0.0 256.5 jit_solution(15304360977704160132)
XLA Ops:
  0.0 8.3 %shard_map.82 = bf16[128,2,32,256]{3,2,1,0:T(8,128)(2,1)} custom-call(bf16[32,256,128]{2,1,0:T(8,128)(2,1)} %pair_ref.7, s32[32,256]{1,0:T(8,128)} %mask_ref.1, f32[3,128]{1,0:T(4,128)} %gain_ref.7, bf16[128,640]{1,0:T(8,128)(2,1)} %w_ref.8), custom_call_target="tpu_custom_call" | custom-call | tf_op jit(solution)/shard_map/pallas_call | solution.py:84
  8.3 58.6 %all_to_all.15 = bf16[128,2,32,256]{3,2,1,0:T(8,128)(2,1)} all-to-all(bf16[128,2,32,256]{3,2,1,0:T(8,128)(2,1)} %shard_map.82), channel_id=1, replica_groups=mesh['rows'=32,'half'=4] {'rows','half'}, dimensions={0} | all-to-all | bytes 8388608 | tf_op jit(solution)/shard_map/all_to_all | solution.py:440
  66.9 6.1 %shard_map.83 = bf16[32,4,32,256]{3,2,1,0:T(8,128)(2,1)} custom-call(bf16[32,4,2,32,256]{4,3,2,1,0:T(8,128)(2,1)} %bitcast.11), custom_call_target="tpu_custom_call" | custom-call | tf_op jit(solution)/shard_map/pallas_call | solution.py:150
  73.0 9.1 %all-to-all-start.1 = ((bf16[128,32,256]{2,1,0:T(8,128)(2,1)}), bf16[128,32,256]{2,1,0:T(8,128)(2,1)}, u32[]{:S(2)}, u32[]{:S(2)}) async-start(bf16[128,32,256]{2,1,0:T(8,128)(2,1)} %bitcast.12), calls=%async_computation.1 | async-start | bytes 4194304 | tf_op jit(solution)/shard_map/all_to_all | solution.py:443
  82.1 0.7 slice_bitcast_fusion
  82.8 0.7 copy.10.gcol_ref
  84.8 5.6 %shard_map.84.gate_ref = bf16[32,256,128]{2,1,0:T(8,128)(2,1)} custom-call(bf16[32,256,128]{2,1,0:T(8,128)(2,1)} %pair_ref.7, f32[3,128]{1,0:T(4,128)} %gain_ref.7, bf16[128,640]{1,0:T(8,128)(2,1)} %w_ref.8), custom_call_target="tpu_custom_call" | custom-call | flops 805306368 | bytes 4194304 | tf_op jit(solution)/shard_map/pallas_call | solution.py:110
  90.4 17.7 %all-to-all-done.1.prod_ref = bf16[128,32,256]{2,1,0:T(8,128)(2,1)} async-done(((bf16[128,32,256]{2,1,0:T(8,128)(2,1)}), bf16[128,32,256]{2,1,0:T(8,128)(2,1)}, u32[]{:S(2)}, u32[]{:S(2)}) %all-to-all-start.1) | async-done | bytes 2097184 | tf_op jit(solution)/shard_map/all_to_all | solution.py:443
  108.1 6.0 %shard_map.85 = (bf16[16,256,128]{2,1,0:T(8,128)(2,1)}, bf16[17,256,128]{2,1,0:T(8,128)(2,1)}, bf16[16,4,256]{2,1,0:T(4,128)(2,1)}) custom-call(bf16[128,32,256]{2,1,0:T(8,128)(2,1)} %all-to-all-done.1.prod_ref, bf16[32,256,128]{2,1,0:T(8,128)(2,1)} %pair_ref.7, bf16[32,256,128]{2,1,0:T(8,128)(2,1)} %shard_map.84.gate_ref, ...), custom_call_target="tpu_custom_call" | custom-call | tf_op jit(solution)/shard_map/pallas_call | solution.py:205
  114.1 0.6 collective-permute-start.1
  114.7 2.6 %collective-permute-start.2 = (bf16[17,256,128]{2,1,0:T(8,128)(2,1)}, bf16[17,256,128]{2,1,0:T(8,128)(2,1)}, u32[]{:S(2)}, u32[]{:S(2)}) collective-permute-start(bf16[17,256,128]{2,1,0:T(8,128)(2,1)} %get-tuple-element.56.refs_0_.refs_9_), channel_id=1, source_target_pairs={{0,3},{1,0},{2,1},{3,2},{4,7},{5,4},{6,5},{7,6},{8,11},{9,8},{10,9... | collective-permute-start | bytes 3342344 | tf_op jit(solution)/shard_map/ppermute | solution.py:456
  117.3 6.0 %shard_map.86 = (bf16[16,256,128]{2,1,0:T(8,128)(2,1)}, bf16[17,256,128]{2,1,0:T(8,128)(2,1)}, bf16[16,4,256]{2,1,0:T(4,128)(2,1)}) custom-call(bf16[128,32,256]{2,1,0:T(8,128)(2,1)} %all-to-all-done.1.prod_ref, bf16[32,256,128]{2,1,0:T(8,128)(2,1)} %pair_ref.7, bf16[32,256,128]{2,1,0:T(8,128)(2,1)} %shard_map.84.gate_ref, ...), custom_call_target="tpu_custom_call" | custom-call | tf_op jit(solution)/shard_map/pallas_call | solution.py:205
  123.3 0.8 maximum_bitcast_fusion
  124.1 3.4 %collective-permute-start = (bf16[4,32,256]{2,0,1:T(4,128)(2,1)S(1)}, bf16[4,32,256]{2,0,1:T(4,128)(2,1)S(1)}, u32[]{:S(2)}, u32[]{:S(2)}) collective-permute-start(bf16[4,32,256]{2,0,1:T(4,128)(2,1)S(1)} %maximum_bitcast_fusion), channel_id=1, source_target_pairs={{0,0},{1,32},{2,64},{3,96},{4,4},{5,36},{6,68},{7,100},{8,8},{9,40... | collective-permute-start | bytes 196616 | tf_op jit(solution)/shard_map/ppermute | solution.py:469
  127.5 3.8 %shard_map.87 = (bf16[16,256,128]{2,1,0:T(8,128)(2,1)}, bf16[16,256,128]{2,1,0:T(8,128)(2,1)}, bf16[16,256,128]{2,1,0:T(8,128)(2,1)}, bf16[16,256,128]{2,1,0:T(8,128)(2,1)}, f32[16,8,128]{2,1,0:T(8,128)}) custom-call(bf16[128,512]{1,0:T(8,128)(2,1)} %w_ref.13, bf16[17,256,128]{2,1,0:T(8,128)(2,1)} %get-tuple-element.56.refs_0_.refs_9_), custom_call_target="tpu_custom_call" | custom-call | flops 536870912 | bytes 4194304 | tf_op jit(solution)/shard_map/pallas_call | solution.py:282
  131.4 3.8 %shard_map.88 = (bf16[16,256,128]{2,1,0:T(8,128)(2,1)}, bf16[16,256,128]{2,1,0:T(8,128)(2,1)}, bf16[16,256,128]{2,1,0:T(8,128)(2,1)}, bf16[16,256,128]{2,1,0:T(8,128)(2,1)}, f32[16,8,128]{2,1,0:T(8,128)}) custom-call(bf16[128,512]{1,0:T(8,128)(2,1)} %w_ref.13, bf16[17,256,128]{2,1,0:T(8,128)(2,1)} %get-tuple-element.62.refs_0_.refs_7_), custom_call_target="tpu_custom_call" | custom-call | flops 536870912 | bytes 4194304 | tf_op jit(solution)/shard_map/pallas_call | solution.py:282
  135.2 11.1 %collective-permute-done = bf16[4,32,256]{2,0,1:T(4,128)(2,1)S(1)} collective-permute-done((bf16[4,32,256]{2,0,1:T(4,128)(2,1)S(1)}, bf16[4,32,256]{2,0,1:T(4,128)(2,1)S(1)}, u32[]{:S(2)}, u32[]{:S(2)}) %collective-permute-start) | collective-permute-done | bytes 65568 | tf_op jit(solution)/shard_map/ppermute | solution.py:469
  146.3 1.2 broadcast_in_dim.2
  147.5 7.2 %all-to-all-start.2 = ((bf16[16,4,32,256]{3,2,1,0:T(8,128)(2,1)}), bf16[16,4,32,256]{3,2,1,0:T(8,128)(2,1)}, u32[]{:S(2)}, u32[]{:S(2)}) async-start(bf16[16,4,32,256]{3,2,1,0:T(8,128)(2,1)} %broadcast_in_dim.2), calls=%async_computation.2 | async-start | bytes 2097152 | tf_op jit(solution)/shard_map/all_to_all | solution.py:476
  154.7 2.8 %collective-permute-start.4 = (bf16[17,256,128]{2,1,0:T(8,128)(2,1)}, bf16[17,256,128]{2,1,0:T(8,128)(2,1)}, u32[]{:S(2)}, u32[]{:S(2)}) collective-permute-start(bf16[17,256,128]{2,1,0:T(8,128)(2,1)} %get-tuple-element.62.refs_0_.refs_7_), channel_id=1, source_target_pairs={{0,3},{1,0},{2,1},{3,2},{4,7},{5,4},{6,5},{7,6},{8,11},{9,8},{10,9... | collective-permute-start | bytes 3342344 | tf_op jit(solution)/shard_map/ppermute | solution.py:456
  157.5 4.0 %shard_map.89 = (bf16[16,512,128]{2,1,0:T(8,128)(2,1)}, bf16[16,512,128]{2,1,0:T(8,128)(2,1)}, f32[16,8,128]{2,1,0:T(8,128)}) custom-call(bf16[128,512]{1,0:T(8,128)(2,1)} %w_ref.13, bf16[17,256,128]{2,1,0:T(8,128)(2,1)} %copy-done.4, bf16[17,256,128]{2,1,0:T(8,128)(2,1)} %collective-permute-done.2.refs_1_.refs_11_), custom_call_target="tpu_custom_call" | custom-call | flops 1073741824 | bytes 8388608 | tf_op jit(solution)/shard_map/pallas_call | solution.py:282
  161.5 5.4 %all-to-all-done.2 = bf16[16,4,32,256]{3,2,1,0:T(8,128)(2,1)} async-done(((bf16[16,4,32,256]{3,2,1,0:T(8,128)(2,1)}), bf16[16,4,32,256]{3,2,1,0:T(8,128)(2,1)}, u32[]{:S(2)}, u32[]{:S(2)}) %all-to-all-start.2) | async-done | bytes 1048608 | tf_op jit(solution)/shard_map/all_to_all | solution.py:476
  167.1 0.6 pad_add_fusion.me_ref
  167.8 0.7 compare_convert_fusion.refs_1_.refs_3_
  168.5 11.9 %collective-permute-done.4.refs_1_.refs_9_ = bf16[17,256,128]{2,1,0:T(8,128)(2,1)} collective-permute-done((bf16[17,256,128]{2,1,0:T(8,128)(2,1)}, bf16[17,256,128]{2,1,0:T(8,128)(2,1)}, u32[]{:S(2)}, u32[]{:S(2)}) %collective-permute-start.4) | collective-permute-done | bytes 1114144 | tf_op jit(solution)/shard_map/ppermute | solution.py:456
  180.3 3.7 %collective-permute-start.6 = (bf16[17,256,128]{2,1,0:T(8,128)(2,1)}, bf16[17,256,128]{2,1,0:T(8,128)(2,1)}, u32[]{:S(2)}, u32[]{:S(2)}) collective-permute-start(bf16[17,256,128]{2,1,0:T(8,128)(2,1)} %collective-permute-done.4.refs_1_.refs_9_), channel_id=1, source_target_pairs={{0,3},{1,0},{2,1},{3,2},{4,7},{5,4},{6,5},{7,6},{8,11},{9,8},{10,9... | collective-permute-start | bytes 3342344 | tf_op jit(solution)/shard_map/ppermute | solution.py:457
  184.0 2.5 collective-permute-done.7.refs_0_.refs_12_
  186.5 1.1 copy-done
  187.6 3.6 %shard_map.90 = (bf16[16,256,128]{2,1,0:T(8,128)(2,1)}, bf16[16,256,128]{2,1,0:T(8,128)(2,1)}, f32[16,8,128]{2,1,0:T(8,128)}) custom-call(bf16[128,512]{1,0:T(8,128)(2,1)} %w_ref.13, bf16[17,256,128]{2,1,0:T(8,128)(2,1)} %copy-done, bf16[128,128]{1,0:T(8,128)(2,1)} %compare_convert_fusion.refs_1_.refs_3_, ...), custom_call_target="tpu_custom_call" | custom-call | flops 536870912 | bytes 4194304 | tf_op jit(solution)/shard_map/pallas_call | solution.py:282
  191.2 25.3 %shard_map.91.refs_11_ = bf16[32,256,128]{2,1,0:T(8,128)(2,1)} custom-call(s32[2]{0:T(128)} %pad_add_fusion.me_ref, bf16[4,4,4,32,256]{4,3,2,1,0:T(8,128)(2,1)} %bitcast.7.bias_a_ref, bf16[4,4,4,32,256]{4,3,2,1,0:T(8,128)(2,1)} %bitcast.8.bias_b_ref, bf16[128,128]{1,0:T(8,128)(2,1)} %wo_ref.7, f32[16,8,128]{2,1,0:T(8,128)} %get-tuple-element.81.reach_ref, ...), custom_call_target="tpu_custom_call" | custom-call | flops 34359738368 | bytes 16777216 | tf_op jit(solution)/shard_map/pallas_call | solution.py:408
  216.5 14.7 %shard_map.92 = (bf16[16,768,128]{2,1,0:T(8,128)(2,1)}, bf16[16,768,128]{2,1,0:T(8,128)(2,1)}, f32[16,8,128]{2,1,0:T(8,128)}) custom-call(bf16[128,512]{1,0:T(8,128)(2,1)} %w_ref.13, bf16[17,256,128]{2,1,0:T(8,128)(2,1)} %collective-permute-done.5.refs_0_.refs_8_, bf16[17,256,128]{2,1,0:T(8,128)(2,1)} %collective-permute-done.4.refs_1_.refs_9_, ...), custom_call_target="tpu_custom_call" | custom-call | flops 1610612736 | bytes 12582912 | tf_op jit(solution)/shard_map/pallas_call | solution.py:282
  231.2 25.1 %shard_map.93 = bf16[32,256,128]{2,1,0:T(8,128)(2,1)} custom-call(s32[2]{0:T(128)} %pad_add_fusion.me_ref, bf16[4,4,4,32,256]{4,3,2,1,0:T(8,128)(2,1)} %bitcast.7.bias_a_ref, bf16[4,4,4,32,256]{4,3,2,1,0:T(8,128)(2,1)} %bitcast.8.bias_b_ref, bf16[128,128]{1,0:T(8,128)(2,1)} %wo_ref.7, ...), custom_call_target="tpu_custom_call", output_to_operand_aliasing={{}: (16, {})} | custom-call | flops 34359738368 | bytes 16777216 | tf_op jit(solution)/shard_map/pallas_call | solution.py:408
  (22 shorter events, 1.5 us)
Async XLA Ops:
  73.0 9.1 %copy-start.1 = (s32[32,256]{1,0:T(8,128)S(1)}, s32[32,256]{1,0:T(8,128)}, u32[]{:S(2)}) copy-start(s32[32,256]{1,0:T(8,128)} %mask_ref.1) | copy-start | bytes 98308
  73.0 11.2 %copy-start.3 = (bf16[128,4]{0,1:T(4,128)(2,1)S(1)}, bf16[128,4]{0,1:T(4,128)(2,1)}, u32[]{:S(2)}) copy-start(bf16[128,4]{0,1:T(4,128)(2,1)} %param.14) | copy-start | bytes 3076
  73.0 35.1 %all-to-all-start.1 = ((bf16[128,32,256]{2,1,0:T(8,128)(2,1)}), bf16[128,32,256]{2,1,0:T(8,128)(2,1)}, u32[]{:S(2)}, u32[]{:S(2)}) async-start(bf16[128,32,256]{2,1,0:T(8,128)(2,1)} %bitcast.12), calls=%async_computation.1 | async-start | bytes 4194304 | tf_op jit(solution)/shard_map/all_to_all | solution.py:443
  114.1 9.2 %copy-start.2 = (bf16[16,4,256]{2,1,0:T(4,128)(2,1)S(1)}, bf16[16,4,256]{2,1,0:T(4,128)(2,1)}, u32[]{:S(2)}) copy-start(bf16[16,4,256]{2,1,0:T(4,128)(2,1)} %get-tuple-element.54) | copy-start | bytes 98308
  114.1 32.2 %collective-permute-start.1 = (bf16[17,256,128]{2,1,0:T(8,128)(2,1)}, bf16[17,256,128]{2,1,0:T(8,128)(2,1)S(1)}, u32[]{:S(2)}, u32[]{:S(2)}) collective-permute-start(bf16[17,256,128]{2,1,0:T(8,128)(2,1)} %get-tuple-element.56.refs_0_.refs_9_), channel_id=1, source_target_pairs={{0,1},{1,2},{2,3},{3,0},{4,5},{5,6},{6,7},{7,4},{8,9},{9,10},{10,1... | collective-permute-start | bytes 3342344 | tf_op jit(solution)/shard_map/ppermute | solution.py:455
  114.7 31.6 %collective-permute-start.2 = (bf16[17,256,128]{2,1,0:T(8,128)(2,1)}, bf16[17,256,128]{2,1,0:T(8,128)(2,1)}, u32[]{:S(2)}, u32[]{:S(2)}) collective-permute-start(bf16[17,256,128]{2,1,0:T(8,128)(2,1)} %get-tuple-element.56.refs_0_.refs_9_), channel_id=1, source_target_pairs={{0,3},{1,0},{2,1},{3,2},{4,7},{5,4},{6,5},{7,6},{8,11},{9,8},{10,9... | collective-permute-start | bytes 3342344 | tf_op jit(solution)/shard_map/ppermute | solution.py:456
  124.1 22.2 %collective-permute-start = (bf16[4,32,256]{2,0,1:T(4,128)(2,1)S(1)}, bf16[4,32,256]{2,0,1:T(4,128)(2,1)S(1)}, u32[]{:S(2)}, u32[]{:S(2)}) collective-permute-start(bf16[4,32,256]{2,0,1:T(4,128)(2,1)S(1)} %maximum_bitcast_fusion), channel_id=1, source_target_pairs={{0,0},{1,32},{2,64},{3,96},{4,4},{5,36},{6,68},{7,100},{8,8},{9,40... | collective-permute-start | bytes 196616 | tf_op jit(solution)/shard_map/ppermute | solution.py:469
  146.3 8.4 %copy-start.4 = (bf16[17,256,128]{2,1,0:T(8,128)(2,1)}, bf16[17,256,128]{2,1,0:T(8,128)(2,1)S(1)}, u32[]{:S(2)}) copy-start(bf16[17,256,128]{2,1,0:T(8,128)(2,1)S(1)} %collective-permute-done.1.refs_0_.refs_10_) | copy-start | bytes 3342340
  147.5 19.4 %all-to-all-start.2 = ((bf16[16,4,32,256]{3,2,1,0:T(8,128)(2,1)}), bf16[16,4,32,256]{3,2,1,0:T(8,128)(2,1)}, u32[]{:S(2)}, u32[]{:S(2)}) async-start(bf16[16,4,32,256]{3,2,1,0:T(8,128)(2,1)} %broadcast_in_dim.2), calls=%async_computation.2 | async-start | bytes 2097152 | tf_op jit(solution)/shard_map/all_to_all | solution.py:476
  154.7 25.6 %collective-permute-start.4 = (bf16[17,256,128]{2,1,0:T(8,128)(2,1)}, bf16[17,256,128]{2,1,0:T(8,128)(2,1)}, u32[]{:S(2)}, u32[]{:S(2)}) collective-permute-start(bf16[17,256,128]{2,1,0:T(8,128)(2,1)} %get-tuple-element.62.refs_0_.refs_7_), channel_id=1, source_target_pairs={{0,3},{1,0},{2,1},{3,2},{4,7},{5,4},{6,5},{7,6},{8,11},{9,8},{10,9... | collective-permute-start | bytes 3342344 | tf_op jit(solution)/shard_map/ppermute | solution.py:456
  157.5 28.9 %collective-permute-start.7 = (bf16[17,256,128]{2,1,0:T(8,128)(2,1)}, bf16[17,256,128]{2,1,0:T(8,128)(2,1)S(1)}, u32[]{:S(2)}, u32[]{:S(2)}) collective-permute-start(bf16[17,256,128]{2,1,0:T(8,128)(2,1)} %copy-done.4), channel_id=1, source_target_pairs={{0,1},{1,2},{2,3},{3,0},{4,5},{5,6},{6,7},{7,4},{8,9},{9,10},{10,1... | collective-permute-start | bytes 3342344 | tf_op jit(solution)/shard_map/ppermute | solution.py:457
  166.9 24.3 %collective-permute-start.3 = (bf16[16,4,32,256]{3,2,1,0:T(8,128)(2,1)}, bf16[16,4,32,256]{3,2,1,0:T(8,128)(2,1)}, u32[]{:S(2)}, u32[]{:S(2)}) collective-permute-start(bf16[16,4,32,256]{3,2,1,0:T(8,128)(2,1)} %all-to-all-done.2), channel_id=1, source_target_pairs={{0,4},{4,0},{8,12},{12,8},{16,20},{20,16},{24,28},{28,24},{32,36},... | collective-permute-start | bytes 3145736 | tf_op jit(solution)/shard_map/ppermute | solution.py:481
  168.5 48.0 %collective-permute-start.5 = (bf16[17,256,128]{2,1,0:T(8,128)(2,1)}, bf16[17,256,128]{2,1,0:T(8,128)(2,1)}, u32[]{:S(2)}, u32[]{:S(2)}) collective-permute-start(bf16[17,256,128]{2,1,0:T(8,128)(2,1)} %get-tuple-element.62.refs_0_.refs_7_), channel_id=1, source_target_pairs={{0,1},{1,2},{2,3},{3,0},{4,5},{5,6},{6,7},{7,4},{8,9},{9,10},{10,1... | collective-permute-start | bytes 3342344 | tf_op jit(solution)/shard_map/ppermute | solution.py:455
  180.3 36.2 %collective-permute-start.6 = (bf16[17,256,128]{2,1,0:T(8,128)(2,1)}, bf16[17,256,128]{2,1,0:T(8,128)(2,1)}, u32[]{:S(2)}, u32[]{:S(2)}) collective-permute-start(bf16[17,256,128]{2,1,0:T(8,128)(2,1)} %collective-permute-done.4.refs_1_.refs_9_), channel_id=1, source_target_pairs={{0,3},{1,0},{2,1},{3,2},{4,7},{5,4},{6,5},{7,6},{8,11},{9,8},{10,9... | collective-permute-start | bytes 3342344 | tf_op jit(solution)/shard_map/ppermute | solution.py:457
  186.5 1.1 copy-start
